TPU v7x, 256 devices: a whole 4x4x8 slice. The times are simulated.
256 devices in a mesh: tm: 16 (over z, y_hi), gz: 16 (over y_lo, x, core).
Axes of the slice: x: 4, y: 4 (y_hi: 2, y_lo: 2; y = y_hi * 2 + y_lo), z: 8, core: 2. Of those that a mesh axis runs over, the one named last changes fastest.
Arguments:
- latent_start: float32 [8, 64, 8, 128], P(None, 'gz'), may hold values from -33 to 33
- noise_draws: bfloat16 [16, 8, 64, 8, 128], P('tm', None, 'gz'), may hold values from -4 to 4
- time_embed: float32 [16, 32], P('tm'), may hold values from -4 to 4
- step_scale: float32 [16], P('tm'), may hold values from 0.1 to 0.5
- noise_scale: float32 [16], P('tm'), may hold values from 0.05 to 0.3
- w_in: bfloat16 [32, 8, 3, 3, 3], replicated, may hold values from -0.4375 to 0.4375
- b_in: float32 [32], replicated, may hold values from -4 to 4
- gain_in: float32 [32], replicated, may hold values from 0.5 to 1.5
- shift_in: float32 [32], replicated, may hold values from -2 to 2
- w_mid: bfloat16 [32, 32, 3, 3, 3], replicated, may hold values from -0.21875 to 0.21875
- b_mid: float32 [32], replicated, may hold values from -4 to 4
- gain_mid: float32 [32], replicated, may hold values from 0.5 to 1.5
- shift_mid: float32 [32], replicated, may hold values from -2 to 2
- w_out: bfloat16 [8, 32, 3, 3, 3], replicated, may hold values from -0.21875 to 0.21875
- b_out: float32 [8], replicated, may hold values from -1.2 to 1.2
Outputs:
- trajectory: float32 [16, 8, 64, 8, 128], P('tm', None, 'gz')
All inputs are finite; a program needn't handle non-finite values.
Results may differ from a plain program's by a relative error of at most 0.00073.
Values may be sent and summed in bfloat16 or wider, within the bound.
A program may use at most 64 MiB of HBM per device.

v0:
```python
import jax
import jax.numpy as jnp
from jax import lax
from jax.sharding import PartitionSpec as P

FEATURES = 32
GROUPS = 8
SWEEPS = 2


def padded(value, sides, width):
    for axis, dim in sides:
        size, length = (lax.axis_size(axis), value.shape[dim])
        up = [(i, (i + 1) % size) for i in range(size)]
        down = [(j, i) for i, j in up]
        last = lax.slice_in_dim(value, length - width, length, axis=dim)
        first = lax.slice_in_dim(value, 0, width, axis=dim)
        before = lax.ppermute(last, axis, up)
        after = lax.ppermute(first, axis, down)
        value = jnp.concatenate([before, value, after], axis=dim)
    return value


def entering(value, axis, combine, identity):
    size, place = (lax.axis_size(axis), lax.axis_index(axis))
    everything = lax.all_gather(value, axis)
    start = jnp.broadcast_to(jnp.asarray(identity, value.dtype), value.shape)

    def lap(k, before):
        reached = k < place
        new = combine(before, everything[k])
        return jnp.where(reached, new, before)

    return lax.fori_loop(0, size, lap, start)


def periodic_rows(volume):
    volume = jnp.concatenate([volume[:, :, -1:], volume, volume[:, :, :1]], axis=2)
    return jnp.concatenate([volume[..., -1:], volume, volume[..., :1]], axis=3)


def slab_conv(volume, weight, bias_vec):
    result = lax.conv_general_dilated(
        periodic_rows(volume)[None],
        weight,
        (1, 1, 1),
        "VALID",
        dimension_numbers=("NCDHW", "OIDHW", "NCDHW"),
        preferred_element_type=jnp.float32,
    )
    return result[0] + bias_vec[:, None, None, None]


def extend_act(activated):
    return padded(activated, (("gz", 1),), 1)


def group_norm(features_map, margin, gain_vec, shift_vec):
    extent_z = features_map.shape[1]
    interior = features_map[:, margin : extent_z - margin]
    grouped = interior.reshape(GROUPS, -1)
    members = grouped.shape[1] * lax.axis_size("gz")
    group_total = lax.psum(jnp.sum(grouped, axis=1), "gz")
    group_mean = group_total / members
    centered = grouped - group_mean[:, None]
    group_var = lax.psum(jnp.sum(centered * centered, axis=1), "gz") / members
    inv_std = jnp.repeat(lax.rsqrt(group_var + 1e-05), FEATURES // GROUPS)
    offset = jnp.repeat(group_mean, FEATURES // GROUPS)
    factor = inv_std * gain_vec
    return (features_map - offset[:, None, None, None]) * factor[:, None, None, None] + shift_vec[
        :, None, None, None
    ]


def drift_of(current, embed_row, step_row, noise_row, draws_row, params):
    w_in, b_in, gain_in, shift_in, w_mid, b_mid, gain_mid, shift_mid, w_out, b_out = params
    state_low = current.astype(jnp.bfloat16)
    bias_in = b_in + embed_row
    extended = padded(state_low, (("gz", 1),), 1)
    lifted = slab_conv(extended, w_in, bias_in)
    act_first = jax.nn.silu(group_norm(lifted, 0, gain_in, shift_in)).astype(jnp.bfloat16)
    summed = slab_conv(extend_act(act_first), w_mid, b_mid) + lifted
    act_second = jax.nn.silu(group_norm(summed, 0, gain_mid, shift_mid)).astype(jnp.bfloat16)
    predicted = slab_conv(extend_act(act_second), w_out, b_out)
    return step_row * predicted + noise_row * draws_row.astype(jnp.float32)


def add_parts(first_part, second_part):
    return first_part + second_part


def time_prefix(increment):
    result = entering(increment, "tm", add_parts, jnp.zeros_like(increment))
    return result


def shards(
    latent_start,
    noise_draws,
    time_embed,
    step_scale,
    noise_scale,
    w_in,
    b_in,
    gain_in,
    shift_in,
    w_mid,
    b_mid,
    gain_mid,
    shift_mid,
    w_out,
    b_out,
):
    params = (w_in, b_in, gain_in, shift_in, w_mid, b_mid, gain_mid, shift_mid, w_out, b_out)
    embed_row = time_embed[0]
    step_row = step_scale[0]
    noise_row = noise_scale[0]
    draws_row = noise_draws[0]
    current = latent_start
    for sweep_index in range(SWEEPS):
        increment = drift_of(current, embed_row, step_row, noise_row, draws_row, params)
        prefix = time_prefix(increment)
        if sweep_index + 1 < SWEEPS:
            current = latent_start + prefix
    return (latent_start + prefix + increment)[None]


def solution(mesh):
    in_specs = (
        P(None, "gz", None, None),
        P("tm", None, "gz", None, None),
        P("tm", None),
        P("tm"),
        P("tm"),
        P(),
        P(),
        P(),
        P(),
        P(),
        P(),
        P(),
        P(),
        P(),
        P(),
    )
    out_specs = P("tm", None, "gz", None, None)
    return jax.shard_map(shards, mesh=mesh, in_specs=in_specs, out_specs=out_specs, check_vma=False)
```

profile of v0, /device:TPU:1, one launch (start us, length us, event | category | flops | bytes accessed | tf_op | source)
XLA Modules:
  0.0 629.6 jit_solution(6607083357325562147)
XLA Ops:
  24.8 29.3 %psum.56 = f32[8]{0:T(128)S(1)} all-reduce(f32[8]{0:T(128)S(1)} %reduce_sum.97), channel_id=1, replica_groups=mesh['tm'=16,'gz'=16] {'gz'}, use_global_device_ids=true, to_apply=%region_2.0 | all-reduce | flops 8 | bytes 64 | tf_op jit(solution)/shard_map/psum | solution.py:63
  56.9 30.9 %psum.57 = f32[8]{0:T(128)S(1)} all-reduce(f32[8]{0:T(128)S(1)} %reduce_sum.100), channel_id=1, replica_groups=mesh['tm'=16,'gz'=16] {'gz'}, use_global_device_ids=true, to_apply=%region_5.6 | all-reduce | flops 8 | bytes 64 | tf_op jit(solution)/shard_map/psum | solution.py:66
  100.3 5.8 reshape.107
  106.0 6.0 copy.149
  113.1 7.1 %select_reduce_fusion.5 = (f32[32]{0:T(128)S(1)}, f32[4,8,8,17,32]{4,2,3,1,0:T(8,128)}) fusion(pred[8,17]{0,1:T(8,128)(4,1)S(1)} %copy-done.5, f32[4,8,8,17,32]{4,2,3,1,0:T(8,128)S(1)} %get-tuple-element.258, f32[32]{0:T(128)S(1)} %bitcast_add_fusion.4, f32[32]{0:T(128)S(1)} %copy-done.6, bf16[32,32,3,3,3]{1,0,4,3,2:T(8,128)(2,1)S(1)} %copy-done, ...), kind=kOutput, calls=%fused_computation.52 | convolution fusion | flops 243234784 | bytes 1745928 | tf_op jit(solution)/shard_map/conv_general_dilated | solution.py:43
  120.3 29.2 %psum.58 = f32[8]{0:T(128)S(1)} all-reduce(f32[8]{0:T(128)S(1)} %reduce_sum.106), channel_id=1, replica_groups=mesh['tm'=16,'gz'=16] {'gz'}, use_global_device_ids=true, to_apply=%region_8.9 | all-reduce | flops 8 | bytes 64 | tf_op jit(solution)/shard_map/psum | solution.py:63
  154.2 31.0 %psum.59 = f32[8]{0:T(128)S(1)} all-reduce(f32[8]{0:T(128)S(1)} %reduce_sum.112), channel_id=1, replica_groups=mesh['tm'=16,'gz'=16] {'gz'}, use_global_device_ids=true, to_apply=%region_11.12 | all-reduce | flops 8 | bytes 64 | tf_op jit(solution)/shard_map/psum | solution.py:66
  199.4 5.1 copy.156
  204.6 5.4 fusion.20
  214.7 85.9 %all-gather.3.cloned.1.call-done = f32[16,8,4,8,128]{4,3,2,1,0:T(8,128)} async-done(((f32[1,8,4,8,128]{4,3,2,1,0:T(8,128)}), f32[16,8,4,8,128]{4,3,2,1,0:T(8,128)}) %all-gather.3.cloned.1.call-update) | async-done | bytes 2097168 | tf_op jit(solution)/shard_map/all_gather | solution.py:26
  300.7 15.7 %while.28 = (s32[]{:T(128)}, f32[8,4,8,128]{3,2,1,0:T(8,128)S(1)}, s32[]{:T(128)}, f32[16,8,4,8,128]{4,3,2,1,0:T(8,128)}, s32[]{:T(128)}, /*index=5*/s32[]{:T(128)}) while((s32[]{:T(128)}, f32[8,4,8,128]{3,2,1,0:T(8,128)S(1)}, s32[]{:T(128)}, f32[16,8,4,8,128]{4,3,2,1,0:T(8,128)}, s32[]{:T(128)}, /*index=5*/s32[]{:T(128)}) %tuple.84), condition=%wide.region_13.14_spmd.clone, body=%wide.region_12.13_spmd.clone.sunk | while | flops 98308 | bytes 393309 | solution.py:34
  316.4 5.4 collective-permute-start.6
  331.6 5.0 select_reduce_fusion.3
  336.9 27.3 %psum.60 = f32[8]{0:T(128)S(1)} all-reduce(f32[8]{0:T(128)S(1)} %reduce_sum.115), channel_id=1, replica_groups=mesh['tm'=16,'gz'=16] {'gz'}, use_global_device_ids=true, to_apply=%region_16.17 | all-reduce | flops 8 | bytes 64 | tf_op jit(solution)/shard_map/psum | solution.py:63
  366.9 30.9 %psum.61 = f32[8]{0:T(128)S(1)} all-reduce(f32[8]{0:T(128)S(1)} %reduce_sum.145), channel_id=1, replica_groups=mesh['tm'=16,'gz'=16] {'gz'}, use_global_device_ids=true, to_apply=%region_19.20 | all-reduce | flops 8 | bytes 64 | tf_op jit(solution)/shard_map/psum | solution.py:66
  410.3 5.8 reshape.130
  416.0 6.0 copy.170
  423.0 7.1 %select_reduce_fusion.1 = (f32[32]{0:T(128)S(1)}, f32[4,8,8,17,32]{4,2,3,1,0:T(8,128)}) fusion(pred[8,17]{0,1:T(8,128)(4,1)S(1)} %copy-done.5, f32[4,8,8,17,32]{4,2,3,1,0:T(8,128)S(1)} %get-tuple-element.262, f32[32]{0:T(128)S(1)} %bitcast_add_fusion.4, f32[32]{0:T(128)S(1)} %copy-done.6, bf16[32,32,3,3,3]{1,0,4,3,2:T(8,128)(2,1)S(1)} %copy-done, ...), kind=kOutput, calls=%fused_computation.47 | convolution fusion | flops 243234784 | bytes 1745928 | tf_op jit(solution)/shard_map/conv_general_dilated | solution.py:43
  430.3 29.2 %psum.62 = f32[8]{0:T(128)S(1)} all-reduce(f32[8]{0:T(128)S(1)} %reduce_sum.148), channel_id=1, replica_groups=mesh['tm'=16,'gz'=16] {'gz'}, use_global_device_ids=true, to_apply=%region_22.23 | all-reduce | flops 8 | bytes 64 | tf_op jit(solution)/shard_map/psum | solution.py:63
  464.2 31.0 %psum.63 = f32[8]{0:T(128)S(1)} all-reduce(f32[8]{0:T(128)S(1)} %reduce_sum.151), channel_id=1, replica_groups=mesh['tm'=16,'gz'=16] {'gz'}, use_global_device_ids=true, to_apply=%region_25.26 | all-reduce | flops 8 | bytes 64 | tf_op jit(solution)/shard_map/psum | solution.py:66
  509.2 5.1 copy.177
  514.4 5.3 fusion.28
  524.6 81.1 %all-gather.5.cloned.1.call-done = f32[16,8,4,8,128]{4,3,2,1,0:T(8,128)} async-done(((f32[1,8,4,8,128]{4,3,2,1,0:T(8,128)}), f32[16,8,4,8,128]{4,3,2,1,0:T(8,128)}) %all-gather.5.cloned.1.call-update) | async-done | bytes 2097168 | tf_op jit(solution)/shard_map/all_gather | solution.py:26
  605.8 15.7 %while.29 = (s32[]{:T(128)}, f32[8,4,8,128]{3,2,1,0:T(8,128)S(1)}, s32[]{:T(128)}, f32[16,8,4,8,128]{4,3,2,1,0:T(8,128)}, s32[]{:T(128)}, /*index=5*/s32[]{:T(128)}) while((s32[]{:T(128)}, f32[8,4,8,128]{3,2,1,0:T(8,128)S(1)}, s32[]{:T(128)}, f32[16,8,4,8,128]{4,3,2,1,0:T(8,128)}, s32[]{:T(128)}, /*index=5*/s32[]{:T(128)}) %tuple.87), condition=%wide.region_27.28_spmd.clone, body=%wide.region_26.27_spmd.clone.sunk | while | flops 98308 | bytes 393309 | solution.py:34
  (237 shorter events, 138.3 us)
Async XLA Ops:
  6.5 106.5 %copy-start = (bf16[32,32,3,3,3]{1,0,4,3,2:T(8,128)(2,1)S(1)}, bf16[32,32,3,3,3]{1,0,4,3,2:T(8,128)(2,1)}, u32[]{:S(2)}) copy-start(bf16[32,32,3,3,3]{1,0,4,3,2:T(8,128)(2,1)} %param.28) | copy-start | bytes 165892
  6.5 294.1 %all-gather.3.cloned.1.call-start = ((), (), s32[]{:S(2)}) async-start(), calls=%async_computation | async-start | bytes 2228224 | tf_op jit(solution)/shard_map/all_gather | solution.py:26
  7.5 4.1 collective-permute-start
  10.2 3.2 collective-permute-start.1
  14.2 5.4 copy-start.5
  14.2 5.4 copy-start.11
  91.0 2.4 copy-start.9
  93.8 1.5 collective-permute-start.2
  93.9 4.0 collective-permute-start.3
  106.0 7.0 %copy-start.6 = (f32[32]{0:T(128)S(1)}, f32[32]{0:T(128)}, u32[]{:S(2)}) copy-start(f32[32]{0:T(128)} %param.29) | copy-start | bytes 388
  189.6 2.5 collective-permute-start.4
  189.7 4.2 collective-permute-start.5
  199.4 5.1 copy-start.12
  209.9 2.9 copy-start.7
  210.0 2.9 copy-start.8
  213.3 103.1 %copy-start.3 = (f32[8,4,8,128]{3,2,1,0:T(8,128)S(1)}, f32[8,4,8,128]{3,2,1,0:T(8,128)}, u32[]{:S(2)}) copy-start(f32[8,4,8,128]{3,2,1,0:T(8,128)} %param.19) | copy-start | bytes 393220
  214.7 391.1 %all-gather.5.cloned.1.call-start = ((), (), s32[]{:S(2)}) async-start(), calls=%async_computation.1 | async-start | bytes 2228224 | tf_op jit(solution)/shard_map/all_gather | solution.py:26
  316.4 6.3 collective-permute-start.6
  321.8 3.6 collective-permute-start.7
  403.8 1.5 collective-permute-start.8
  403.9 4.0 collective-permute-start.9
  499.5 1.5 collective-permute-start.10
  499.6 4.0 collective-permute-start.11
  509.2 5.1 copy-start.13
  (6 other events, 10.8 us)
Sparse Core Ops, SparseCore 0:
  214.8 85.8 all-gather.2
  524.2 81.5 all-gather.4
where the time goes:
time: 642 us; the launch traced here: 630 us
  blocking collectives  239 us (37%)
  waiting for transfers between devices  183 us (29%)
  local copies, waits for them, and re-layouts  97.9 us (15%)
  other arithmetic  45.1 us (7%)
  matrix products  34.8 us (5%)
  between operations  15.9 us (2%)
  starting transfers between devices  13.3 us (2%)
    all_gather x2, waiting for transfers between devices, entering(): everything = lax.all_gather(value, axis)  167 us
    psum x4, blocking collectives, group_norm(): group_var = lax.psum(jnp.sum(centered * centered, axis=1), 'gz') / members  124 us
    psum x4, blocking collectives, group_norm(): group_total = lax.psum(jnp.sum(grouped, axis=1), 'gz')  115 us
    conv_general_dilated x30, local copies, waits for them, and re-layouts, slab_conv(): lax.conv_general_dilated(periodic_rows(volume)[None], weight, (1, 1, 1),...  74.9 us
    conv_general_dilated x6, matrix products, slab_conv(): lax.conv_general_dilated(periodic_rows(volume)[None], weight, (1, 1, 1),...  34.8 us
    select_n x32, other arithmetic, lap(): return jnp.where(reached, new, before)  30.6 us
    ppermute x6, waiting for transfers between devices, padded(): after = lax.ppermute(first, axis, down)  14.1 us
    unnamed x44, local copies, waits for them, and re-layouts  13.2 us
  transfers between devices with their start and end apart: 14, of which 12 were waited for; matrix products, arithmetic and copies ran while one was open for 0% of the time, Pallas kernels for 0%

commit v1 on v0

v1 whole, which is shorter than its diff:
```python
import functools

import jax
import jax.numpy as jnp
from jax import lax
from jax.experimental import pallas as pl
from jax.experimental.pallas import tpu as pltpu
from jax.sharding import PartitionSpec as P

MESH = pl.DeviceIdType.MESH
F32, BF16 = jnp.float32, jnp.bfloat16
CH, FT, GR = 8, 32, 8
NY, NX, NZ = 8, 128, 4
SIDE = 16
HALO = 3
CELLS = (FT // GR) * NZ * NY * NX

GZ_ORDER = (12, 13, 4, 5, 8, 9, 14, 15, 10, 11, 2, 3, 6, 7, 1)
TM_ORDER = (
    (4, 1), (3, 1), (5, 1), (4, 0), (2, 1), (6, 1), (3, 0), (5, 0),
    (1, 1), (7, 1), (2, 0), (6, 0), (0, 1), (1, 0), (7, 0),
)


def flip(place, bits):
    for bit in (1, 2, 4, 8):
        if bits & bit:
            place = place + bit - 2 * bit * lax.rem(lax.div(place, bit), 2)
    return place


def shifted(place, steps, other):
    z, half = lax.div(place, 2), lax.rem(place, 2)
    if other:
        half = 1 - half
    return 2 * lax.rem(z + steps, SIDE // 2) + half


def unfold(count):
    row = lax.broadcasted_iota(jnp.int32, (count, 8 * count), 0)
    lane = lax.broadcasted_iota(jnp.int32, (count, 8 * count), 1)
    return (lax.div(lane, 8) == row).astype(F32).astype(BF16)


def tap_masks(lanes):
    y = lax.broadcasted_iota(jnp.int32, (8, lanes), 0)
    yin = lax.rem(lax.broadcasted_iota(jnp.int32, (8, lanes), 1), 8)
    return [yin == lax.rem(y + b + 7, 8) for b in range(3)]


def circulant(rows, masks):
    n, lanes = rows[0].shape
    out = jnp.zeros((n, 8, lanes), F32)
    for row, mask in zip(rows, masks):
        full = jnp.broadcast_to(row[:, None, :], (n, 8, lanes))
        out = jnp.where(jnp.broadcast_to(mask[None], (n, 8, lanes)), full, out)
    return out.reshape(8 * n, lanes)


def kernel(
    lat_ref, noise_ref, emb_ref, step_ref, nsc_ref, win_ref, bin_ref, gin_ref, sin_ref,
    wmid_ref, bmid_ref, gmid_ref, smid_ref, wout_ref, bout_ref,
    out_ref,
    vext, shift_in, lifted, act, summed, actb, a_in, a_mid, a_out, x_mid, splat, splat_out,
    stat, recv, send1, lat_chunk, chunk_a, chunk_b,
    halo_ss, halo_rs, stat_ss, stat_rs, p1_ss, p1_rs, p2_ss, p2_rs,
):
    k = lax.axis_index("tm")
    g = lax.axis_index("gz")
    up, down = lax.rem(g + 1, SIDE), lax.rem(g + SIDE - 1, SIDE)
    gz_peers = [flip(g, bits) for bits in GZ_ORDER]
    tm_peers = [shifted(k, steps, other) for steps, other in TM_ORDER]
    my_z, my_p = lax.div(k, 4), lax.rem(k, 4)
    pending = []

    barrier = pltpu.get_barrier_semaphore()
    for peer in tm_peers:
        pl.semaphore_signal(barrier, inc=1, device_id={"tm": peer}, device_id_type=MESH)
    for peer in gz_peers:
        pl.semaphore_signal(barrier, inc=1, device_id={"gz": peer}, device_id_type=MESH)

    for z in range(NZ):
        plane = lat_ref[:, z].reshape(CH * NY, NX)
        vext[0, HALO + z] = plane.reshape(4, 16, NX).astype(BF16)
        lat_chunk[4 * z : 4 * z + 4] = plane.reshape(4, 2, NY, NX)

    def mid_rows():
        x_mid[...] = jnp.dot(wmid_ref[...], unfold(FT), preferred_element_type=F32)
        masks = tap_masks(256)
        for a in range(3):
            for block in range(12):
                rows = [x_mid[(a * 3 + b) * 96 + 8 * block : (a * 3 + b) * 96 + 8 * block + 8, :] for b in range(3)]
                a_mid[64 * block : 64 * block + 64, 256 * a : 256 * a + 256] = circulant(rows, masks).astype(BF16)

    mid_rows()
    masks = tap_masks(256)
    x_out = jnp.dot(wout_ref[...], unfold(FT), preferred_element_type=F32)
    for a in range(3):
        rows = [x_out[(a * 3 + b) * 24 : (a * 3 + b) * 24 + 24] for b in range(3)]
        a_out[:, 256 * a : 256 * a + 256] = circulant(rows, masks).astype(BF16)
    masks = tap_masks(576)
    rows = []
    for b in range(3):
        w_b = jnp.concatenate([win_ref[(a * 3 + b) * 24 : (a * 3 + b) * 24 + 24, :].astype(F32) for a in range(3)], axis=0)
        rows.append(jnp.dot(w_b.T.astype(BF16), unfold(72), preferred_element_type=F32))
    for block in range(4):
        part = [row[8 * block : 8 * block + 8] for row in rows]
        a_in[64 * block : 64 * block + 64, :] = circulant(part, masks).astype(BF16)

    def spread(o, carry):
        at = pl.ds(o * 8 if isinstance(o, int) else pl.multiple_of(o * 8, 8), 8)
        for i, value in enumerate((
            bin_ref[o] + emb_ref[0, o], gin_ref[o], sin_ref[o], bmid_ref[o], gmid_ref[o], smid_ref[o],
        )):
            splat[i, at, :] = jnp.full((8, NX), value, F32)
        return carry

    lax.fori_loop(0, FT, spread, 0)
    for o in range(CH):
        splat_out[8 * o : 8 * o + 8, :] = jnp.full((8, NX), bout_ref[o], F32)

    pl.semaphore_wait(barrier, 2 * (SIDE - 1))

    def send(src, dst, ss, rs, device):
        copy = pltpu.make_async_remote_copy(
            src_ref=src, dst_ref=dst, send_sem=ss, recv_sem=rs, device_id=device, device_id_type=MESH
        )
        copy.start()
        pending.append(copy)
        return copy

    def halos(sweep):
        copies = [
            send(vext.at[sweep, pl.ds(NZ, HALO)], vext.at[sweep, pl.ds(0, HALO)],
                 halo_ss.at[sweep, 0], halo_rs.at[sweep, 0], {"gz": up}),
            send(vext.at[sweep, pl.ds(HALO, HALO)], vext.at[sweep, pl.ds(HALO + NZ, HALO)],
                 halo_ss.at[sweep, 1], halo_rs.at[sweep, 1], {"gz": down}),
        ]
        for copy in copies:
            copy.wait_recv()

    sub = lax.broadcasted_iota(jnp.int32, (8, NX), 0)
    low = lax.broadcasted_iota(jnp.int32, (8, NX), 1) < NX // 2

    def group_totals(ref, first, centre):
        totals = []
        for gr in range(GR):
            part = ref[32 * gr : 32 * gr + 32, first : first + NZ * NX]
            if centre is not None:
                part = part - centre[gr]
                part = part * part
            part = part.reshape(4, 8, NZ * NX)
            part = part[0] + part[1] + part[2] + part[3]
            part = part[:, :128] + part[:, 128:256] + part[:, 256:384] + part[:, 384:]
            part = jnp.sum(part, axis=0, keepdims=True)
            totals.append(jnp.sum(part, axis=1, keepdims=True))
        return totals

    def statistics(ref, first, turn):
        means = [t * (1.0 / CELLS) for t in group_totals(ref, first, None)]
        squares = group_totals(ref, first, means)
        tile = jnp.zeros((8, NX), F32)
        for gr in range(GR):
            both = jnp.where(low, jnp.broadcast_to(means[gr], (8, NX)), jnp.broadcast_to(squares[gr], (8, NX)))
            tile = jnp.where(sub == gr, both, tile)
        stat[turn] = tile
        recv[turn, g] = tile
        copies = []
        for i, peer in enumerate(gz_peers):
            copies.append(send(stat.at[turn], recv.at[turn, g], stat_ss.at[turn, i], stat_rs.at[turn, i], {"gz": peer}))
        for copy in copies:
            copy.wait_recv()
        every = recv[turn]
        total = jnp.sum(every, axis=0)
        mean = total * (1.0 / SIDE)
        off = every - mean[None]
        spread_of = jnp.sum(off * off, axis=0)
        var = (pltpu.roll(total, NX // 2, 1) + spread_of * CELLS) * (1.0 / (CELLS * SIDE))
        inv = lax.rsqrt(var + 1e-05)
        return jnp.where(low, mean, pltpu.roll(mean, NX // 2, 1)), jnp.where(low, inv, pltpu.roll(inv, NX // 2, 1))

    def normed(ref, gr, mean, inv, gain, shift):
        rows = ref[32 * gr : 32 * gr + 32, :]
        lanes = rows.shape[1]
        at = slice(32 * gr, 32 * gr + 32)
        m = jnp.broadcast_to(mean[gr : gr + 1], (32, NX))
        f = jnp.broadcast_to(inv[gr : gr + 1], (32, NX)) * splat[gain, at, :]
        s = splat[shift, at, :]
        tile = lambda t: jnp.concatenate([t] * (lanes // NX), axis=1)
        value = (rows - tile(m)) * tile(f) + tile(s)
        return value / (1.0 + jnp.exp(-value))

    step, noise_scale = step_ref[0], nsc_ref[0]

    for sweep in range(2):
        halos(sweep)
        for e in range(NZ + 2 * HALO):
            plane = vext[sweep, e].reshape(CH * NY, NX)
            wide = plane.astype(F32)
            at = slice(NX * e, NX * e + NX)
            shift_in[0:64, at] = pltpu.roll(wide, 1, 1).astype(BF16)
            shift_in[64:128, at] = plane
            shift_in[128:192, at] = pltpu.roll(wide, NX - 1, 1).astype(BF16)
        stacked = jnp.concatenate([shift_in[:, NX * a : NX * a + 1024] for a in range(3)], axis=0)
        lifted[...] = jnp.dot(a_in[...], stacked, preferred_element_type=F32) + jnp.concatenate([splat[0]] * 8, axis=1)

        mean, inv = statistics(lifted, 2 * NX, 2 * sweep)
        for gr in range(GR):
            act[32 * gr : 32 * gr + 32, :] = normed(lifted, gr, mean, inv, 1, 2).astype(BF16)
        stacked = jnp.concatenate([act[:, NX * a : NX * a + 768] for a in range(3)], axis=0)
        for part in range(4):
            at = slice(64 * part, 64 * part + 64)
            taps = [
                jnp.dot(a_mid[256 * c + 64 * part : 256 * c + 64 * part + 64, :], stacked, preferred_element_type=F32)
                for c in range(3)
            ]
            for z in range(NZ + 2):
                cut = slice(NX * z, NX * z + NX)
                summed[at, cut] = (
                    pltpu.roll(taps[0][:, cut], 1, 1) + taps[1][:, cut] + pltpu.roll(taps[2][:, cut], NX - 1, 1)
                    + splat[3, at, :] + lifted[at, NX * (z + 1) : NX * (z + 2)]
                )

        mean, inv = statistics(summed, NX, 2 * sweep + 1)
        for gr in range(GR):
            actb[32 * gr : 32 * gr + 32, :] = normed(summed, gr, mean, inv, 4, 5).astype(BF16)
        stacked = jnp.concatenate([actb[:, NX * a : NX * a + 512] for a in range(3)], axis=0)
        taps = jnp.dot(a_out[...], stacked, preferred_element_type=F32)
        for z in range(NZ):
            cut = slice(NX * z, NX * z + NX)
            predicted = (
                pltpu.roll(taps[0:64, cut], 1, 1) + taps[64:128, cut] + pltpu.roll(taps[128:192, cut], NX - 1, 1)
                + splat_out[...]
            )
            draws = noise_ref[:, z].astype(F32).reshape(CH * NY, NX)
            send1[sweep, 4 * z : 4 * z + 4] = (step * predicted + noise_scale * draws).reshape(4, 2, NY, NX)

        chunk_a[sweep, k] = send1[sweep, k]
        copies = []
        for i, peer in enumerate(tm_peers):
            copies.append(send(send1.at[sweep, peer], chunk_a.at[sweep, k], p1_ss.at[sweep, i], p1_rs.at[sweep, i], {"tm": peer}))
        for copy in copies:
            copy.wait_recv()
        state = lat_chunk[k]
        for s in range(SIDE):
            if sweep == 0:
                chunk_b[s] = state.reshape(16, NX).astype(BF16)
                state = state + chunk_a[sweep, s]
            else:
                state = state + chunk_a[sweep, s]
                recv_out = state
                send1[2, s] = recv_out
        copies = []
        for i, peer in enumerate(tm_peers):
            if sweep == 0:
                src, dst = chunk_b.at[peer], vext.at[1, HALO + my_z, my_p]
            else:
                src, dst = send1.at[2, peer], out_ref.at[pl.ds(2 * my_p, 2), my_z]
            copies.append(send(src, dst, p2_ss.at[sweep, i], p2_rs.at[sweep, i], {"tm": peer}))
        if sweep == 0:
            vext[1, HALO + my_z, my_p] = chunk_b[k]
        else:
            out_ref[pl.ds(2 * my_p, 2), my_z] = send1[2, k]
        for copy in copies:
            copy.wait_recv()

    for copy in pending:
        copy.wait_send()


def shards(
    latent_start, noise_draws, time_embed, step_scale, noise_scale, w_in, b_in, gain_in, shift_in,
    w_mid, b_mid, gain_mid, shift_mid, w_out, b_out,
):
    vmem, smem = pl.BlockSpec(memory_space=pltpu.VMEM), pl.BlockSpec(memory_space=pltpu.SMEM)
    dma = pltpu.SemaphoreType.DMA
    out = pl.pallas_call(
        kernel,
        out_shape=jax.ShapeDtypeStruct((CH, NZ, NY, NX), F32),
        in_specs=[vmem, vmem, smem, smem, smem, vmem, smem, smem, smem, vmem, smem, smem, smem, vmem, smem],
        out_specs=vmem,
        scratch_shapes=[
            pltpu.VMEM((2, NZ + 2 * HALO, 4, 16, NX), BF16),
            pltpu.VMEM((192, (NZ + 2 * HALO) * NX), BF16),
            pltpu.VMEM((256, 8 * NX), F32),
            pltpu.VMEM((256, 8 * NX), BF16),
            pltpu.VMEM((256, 6 * NX), F32),
            pltpu.VMEM((256, 6 * NX), BF16),
            pltpu.VMEM((256, 576), BF16),
            pltpu.VMEM((768, 768), BF16),
            pltpu.VMEM((192, 768), BF16),
            pltpu.VMEM((864, 256), F32),
            pltpu.VMEM((6, 256, NX), F32),
            pltpu.VMEM((64, NX), F32),
            pltpu.VMEM((4, 8, NX), F32),
            pltpu.VMEM((4, SIDE, 8, NX), F32),
            pltpu.VMEM((3, SIDE, 2, NY, NX), F32),
            pltpu.VMEM((SIDE, 2, NY, NX), F32),
            pltpu.VMEM((2, SIDE, 2, NY, NX), F32),
            pltpu.VMEM((SIDE, 16, NX), BF16),
            dma((2, 2)), dma((2, 2)), dma((4, SIDE)), dma((4, SIDE)),
            dma((2, SIDE)), dma((2, SIDE)), dma((2, SIDE)), dma((2, SIDE)),
        ],
        compiler_params=pltpu.CompilerParams(
            collective_id=0, has_side_effects=True, vmem_limit_bytes=40 * 2**20
        ),
    )(
        latent_start, noise_draws[0], time_embed, step_scale, noise_scale,
        w_in.transpose(2, 3, 4, 1, 0).reshape(27 * CH, FT), b_in, gain_in, shift_in,
        w_mid.transpose(2, 3, 4, 0, 1).reshape(27 * FT, FT), b_mid, gain_mid, shift_mid,
        w_out.transpose(2, 3, 4, 0, 1).reshape(27 * CH, FT), b_out,
    )
    return out[None]


def solution(mesh):
    in_specs = (
        P(None, "gz", None, None), P("tm", None, "gz", None, None), P("tm", None), P("tm"), P("tm"),
        P(), P(), P(), P(), P(), P(), P(), P(), P(), P(),
    )
    out_specs = P("tm", None, "gz", None, None)
    return jax.shard_map(shards, mesh=mesh, in_specs=in_specs, out_specs=out_specs, check_vma=False)
```

time: 642 us -> 76.3 us (0.12); the launches traced: 630 us -> 75.7 us
  blocking collectives: 239 us -> 0 us
  waiting for transfers between devices: 183 us -> 0 us
  local copies, waits for them, and re-layouts: 97.9 us -> 5.66 us
  Pallas kernels: 0 us -> 68.6 us
  other arithmetic: 45.1 us -> 0 us
  matrix products: 34.8 us -> 0 us
  between operations: 15.9 us -> 1.38 us
  starting transfers between devices: 13.3 us -> 0 us
    psum x8 -> x0, blocking collectives: 239 us -> none  [the longest x4 124 us: group_norm(): group_var = lax.psum(jnp.sum(centered * centered, axis=1), 'gz') / members]
    all_gather x2 -> x0, waiting for transfers between devices: 167 us -> none  [entering(): everything = lax.all_gather(value, axis)]
    conv_general_dilated x30 -> x0, local copies, waits for them, and re-layouts: 74.9 us -> none  [slab_conv(): lax.conv_general_dilated(periodic_rows(volume)[None], weight, (1, 1, 1),...]
    pallas_call x0 -> x1, Pallas kernels: none -> 68.6 us  [shards(): pl.pallas_call(kernel, out_shape=jax.ShapeDtypeStruct((CH, NZ, NY, NX), F...]
    conv_general_dilated x6 -> x0, matrix products: 34.8 us -> none  [slab_conv(): lax.conv_general_dilated(periodic_rows(volume)[None], weight, (1, 1, 1),...]
    select_n x32 -> x0, other arithmetic: 30.6 us -> none  [lap(): return jnp.where(reached, new, before)]
    ppermute x12 -> x0, waiting for transfers between devices: 16.1 us -> none  [the longest x6 14.1 us: padded(): after = lax.ppermute(first, axis, down)]
    ppermute x12 -> x0, starting transfers between devices: 13.3 us -> none  [the longest x6 8.43 us: padded(): before = lax.ppermute(last, axis, up)]
  transfers between devices with their start and end apart: 14 -> 0, of which waited for: 12 -> 0; matrix products, arithmetic and copies ran while one was open for 0% -> 0% of each run, Pallas kernels for 0% -> 0%
where the time goes in v1:
time: 76.3 us; the launch traced here: 75.7 us
  Pallas kernels  68.6 us (90%)
  local copies, waits for them, and re-layouts  5.66 us (7%)
  between operations  1.38 us (2%)
    pallas_call x1, Pallas kernels, shards(): pl.pallas_call(kernel, out_shape=jax.ShapeDtypeStruct((CH, NZ, NY, NX), F...  68.6 us
    unnamed x27, local copies, waits for them, and re-layouts  5.66 us

profile of v1, /device:TPU:1, one launch (start us, length us, event | category | flops | bytes accessed | tf_op | source)
XLA Modules:
  0.0 75.7 jit_solution(13629302837026837182)
XLA Ops:
  1.3 0.0 copy-start.12
  1.3 0.0 copy-start.8
  1.3 0.0 copy-start.9
  1.3 0.0 copy-start.10
  1.3 0.0 copy-start.11
  1.3 0.0 copy-start.5
  1.4 0.0 copy-start.6
  1.4 0.0 copy-start.7
  1.4 0.6 copy-done.12
  2.0 0.0 copy-done.8
  2.0 0.0 copy-done.9
  2.0 0.0 copy-done.10
  2.0 0.0 copy-done.11
  2.0 0.0 copy-done.5
  2.0 0.0 copy-done.6
  2.0 0.0 copy-done.7
  2.1 0.0 copy-start
  2.1 0.9 %copy-done = bf16[32,32,3,3,3]{1,0,4,3,2:T(8,128)(2,1)S(1)} copy-done((bf16[32,32,3,3,3]{1,0,4,3,2:T(8,128)(2,1)S(1)}, bf16[32,32,3,3,3]{1,0,4,3,2:T(8,128)(2,1)}, u32[]{:S(2)}) %copy-start) | copy-done | bytes 55320
  3.0 0.9 %copy-done.1 = f32[8,4,8,128]{3,2,1,0:T(8,128)S(1)} copy-done((f32[8,4,8,128]{3,2,1,0:T(8,128)S(1)}, f32[8,4,8,128]{3,2,1,0:T(8,128)}, u32[]{:S(2)}) %copy-start.1) | copy-done | bytes 131096
  3.9 0.8 %copy-done.2 = bf16[1,8,4,8,128]{4,3,2,1,0:T(8,128)(2,1)S(1)} copy-done((bf16[1,8,4,8,128]{4,3,2,1,0:T(8,128)(2,1)S(1)}, bf16[1,8,4,8,128]{4,3,2,1,0:T(8,128)(2,1)}, u32[]{:S(2)}) %copy-start.2) | copy-done | bytes 65560
  4.7 0.8 %copy-done.3 = bf16[32,8,3,3,3]{0,1,4,3,2:T(8,128)(2,1)S(1)} copy-done((bf16[32,8,3,3,3]{0,1,4,3,2:T(8,128)(2,1)S(1)}, bf16[32,8,3,3,3]{0,1,4,3,2:T(8,128)(2,1)}, u32[]{:S(2)}) %copy-start.3) | copy-done | bytes 13848
  5.6 0.8 %copy-done.4 = bf16[8,32,3,3,3]{1,0,4,3,2:T(8,128)(2,1)S(1)} copy-done((bf16[8,32,3,3,3]{1,0,4,3,2:T(8,128)(2,1)S(1)}, bf16[8,32,3,3,3]{1,0,4,3,2:T(8,128)(2,1)}, u32[]{:S(2)}) %copy-start.4) | copy-done | bytes 13848
  6.4 68.6 %shard_map.145 = f32[8,4,8,128]{3,2,1,0:T(8,128)S(1)} custom-call(f32[8,4,8,128]{3,2,1,0:T(8,128)S(1)} %copy-done.1, bf16[8,4,8,128]{3,2,1,0:T(8,128)(2,1)S(1)} %bitcast.13, f32[1,32]{1,0:T(1,128)S(1)} %copy-done.5, f32[1]{0:T(128)S(6)} %copy.17.step_ref, f32[1]{0:T(128)S(6)} %copy.18.nsc_ref, bf16[216,32]{1,0:T(8,128)(2,1)S(1)} %bitcast.14, ...), custom_call_target="tpu_custom_call" | custom-call | tf_op jit(solution)/shard_map/pallas_call | solution.py:277
  75.0 0.7 copy.19
  (4 shorter events, 0.0 us)
Async XLA Ops:
  1.3 0.7 copy-start.12
  1.3 0.7 copy-start.8
  1.3 0.7 copy-start.9
  1.3 0.7 copy-start.10
  1.3 0.7 copy-start.11
  1.3 0.7 copy-start.5
  1.4 0.7 copy-start.6
  1.4 0.7 copy-start.7
  2.1 0.9 %copy-start = (bf16[32,32,3,3,3]{1,0,4,3,2:T(8,128)(2,1)S(1)}, bf16[32,32,3,3,3]{1,0,4,3,2:T(8,128)(2,1)}, u32[]{:S(2)}) copy-start(bf16[32,32,3,3,3]{1,0,4,3,2:T(8,128)(2,1)} %param.24) | copy-start | bytes 165892
  3.0 0.9 %copy-start.1 = (f32[8,4,8,128]{3,2,1,0:T(8,128)S(1)}, f32[8,4,8,128]{3,2,1,0:T(8,128)}, u32[]{:S(2)}) copy-start(f32[8,4,8,128]{3,2,1,0:T(8,128)} %lat_ref.1) | copy-start | bytes 393220
  3.9 0.8 %copy-start.2 = (bf16[1,8,4,8,128]{4,3,2,1,0:T(8,128)(2,1)S(1)}, bf16[1,8,4,8,128]{4,3,2,1,0:T(8,128)(2,1)}, u32[]{:S(2)}) copy-start(bf16[1,8,4,8,128]{4,3,2,1,0:T(8,128)(2,1)} %param.16) | copy-start | bytes 196612
  4.7 0.8 %copy-start.3 = (bf16[32,8,3,3,3]{0,1,4,3,2:T(8,128)(2,1)S(1)}, bf16[32,8,3,3,3]{0,1,4,3,2:T(8,128)(2,1)}, u32[]{:S(2)}) copy-start(bf16[32,8,3,3,3]{0,1,4,3,2:T(8,128)(2,1)} %param.20) | copy-start | bytes 41476
  5.6 0.8 %copy-start.4 = (bf16[8,32,3,3,3]{1,0,4,3,2:T(8,128)(2,1)S(1)}, bf16[8,32,3,3,3]{1,0,4,3,2:T(8,128)(2,1)}, u32[]{:S(2)}) copy-start(bf16[8,32,3,3,3]{1,0,4,3,2:T(8,128)(2,1)} %param.28) | copy-start | bytes 41476

commit v2 on v1

v2 whole, which is shorter than its diff:
```python
import functools

import jax
import jax.numpy as jnp
from jax import lax
from jax.experimental import pallas as pl
from jax.experimental.pallas import tpu as pltpu
from jax.sharding import PartitionSpec as P

MESH = pl.DeviceIdType.MESH
F32, BF16 = jnp.float32, jnp.bfloat16
CH, FT, GR = 8, 32, 8
NY, NX, NZ = 8, 128, 4
SIDE = 16
HALO = 3
CELLS = (FT // GR) * NZ * NY * NX

GZ_ORDER = (12, 13, 4, 5, 8, 9, 14, 15, 10, 11, 2, 3, 6, 7, 1)
TM_ORDER = (
    (4, 1), (3, 1), (5, 1), (4, 0), (2, 1), (6, 1), (3, 0), (5, 0),
    (1, 1), (7, 1), (2, 0), (6, 0), (0, 1), (1, 0), (7, 0),
)


def flip(place, bits):
    for bit in (1, 2, 4, 8):
        if bits & bit:
            place = place + bit - 2 * bit * lax.rem(lax.div(place, bit), 2)
    return place


def shifted(place, steps, other):
    z, half = lax.div(place, 2), lax.rem(place, 2)
    if other:
        half = 1 - half
    return 2 * lax.rem(z + steps, SIDE // 2) + half


def unfold(count):
    row = lax.broadcasted_iota(jnp.int32, (count, 8 * count), 0)
    lane = lax.broadcasted_iota(jnp.int32, (count, 8 * count), 1)
    return (lax.div(lane, 8) == row).astype(F32).astype(BF16)


def tap_masks(lanes):
    y = lax.broadcasted_iota(jnp.int32, (8, lanes), 0)
    yin = lax.rem(lax.broadcasted_iota(jnp.int32, (8, lanes), 1), 8)
    return [yin == lax.rem(y + b + 7, 8) for b in range(3)]


def circulant(rows, masks):
    n, lanes = rows[0].shape
    out = jnp.zeros((n, 8, lanes), F32)
    for row, mask in zip(rows, masks):
        full = jnp.broadcast_to(row[:, None, :], (n, 8, lanes))
        out = jnp.where(jnp.broadcast_to(mask[None], (n, 8, lanes)), full, out)
    return out.reshape(8 * n, lanes)


def kernel(
    lat_hbm, noise_hbm, emb_hbm, step_hbm, nsc_hbm, win_hbm, bin_hbm, gin_hbm, sin_hbm,
    wmid_hbm, bmid_hbm, gmid_hbm, smid_hbm, wout_hbm, bout_hbm,
    out_ref,
    lat_ref, noise_ref, win_ref, wmid_ref, wout_ref, emb_ref, step_ref, nsc_ref,
    bin_ref, gin_ref, sin_ref, bmid_ref, gmid_ref, smid_ref, bout_ref,
    vext, shift_in, lifted, act, summed, actb, a_in, a_mid, a_out, x_mid, splat, splat_out,
    stat, recv, send1, lat_chunk, chunk_a, chunk_b,
    load_sem, halo_ss, halo_rs, stat_ss, stat_rs, p1_ss, p1_rs, p2_ss, p2_rs,
):
    k = lax.axis_index("tm")
    g = lax.axis_index("gz")
    up, down = lax.rem(g + 1, SIDE), lax.rem(g + SIDE - 1, SIDE)
    gz_peers = [flip(g, bits) for bits in GZ_ORDER]
    tm_peers = [shifted(k, steps, other) for steps, other in TM_ORDER]
    my_z, my_p = lax.div(k, 4), lax.rem(k, 4)
    pending = []

    barrier = pltpu.get_barrier_semaphore()
    for peer in tm_peers:
        pl.semaphore_signal(barrier, inc=1, device_id={"tm": peer}, device_id_type=MESH)
    for peer in gz_peers:
        pl.semaphore_signal(barrier, inc=1, device_id={"gz": peer}, device_id_type=MESH)

    loads = []
    for src, dst in (
        (lat_hbm, lat_ref), (wmid_hbm, wmid_ref), (wout_hbm, wout_ref), (win_hbm, win_ref), (emb_hbm, emb_ref),
        (bin_hbm, bin_ref), (gin_hbm, gin_ref), (sin_hbm, sin_ref), (bmid_hbm, bmid_ref), (gmid_hbm, gmid_ref),
        (smid_hbm, smid_ref), (bout_hbm, bout_ref), (step_hbm, step_ref), (nsc_hbm, nsc_ref), (noise_hbm, noise_ref),
    ):
        copy = pltpu.make_async_copy(src, dst, load_sem.at[len(loads)])
        copy.start()
        loads.append(copy)

    loads[0].wait()
    for z in range(NZ):
        plane = lat_ref[:, z].reshape(CH * NY, NX)
        vext[0, HALO + z] = plane.reshape(4, 16, NX).astype(BF16)
        lat_chunk[4 * z : 4 * z + 4] = plane.reshape(4, 2, NY, NX)

    loads[1].wait()
    x_mid[...] = jnp.dot(wmid_ref[...], unfold(FT), preferred_element_type=F32)
    masks = tap_masks(256)
    for a in range(3):
        for block in range(12):
            rows = [x_mid[(a * 3 + b) * 96 + 8 * block : (a * 3 + b) * 96 + 8 * block + 8, :] for b in range(3)]
            a_mid[64 * block : 64 * block + 64, 256 * a : 256 * a + 256] = circulant(rows, masks).astype(BF16)
    loads[2].wait()
    x_out = jnp.dot(wout_ref[...], unfold(FT), preferred_element_type=F32)
    for a in range(3):
        rows = [x_out[(a * 3 + b) * 24 : (a * 3 + b) * 24 + 24] for b in range(3)]
        a_out[:, 256 * a : 256 * a + 256] = circulant(rows, masks).astype(BF16)
    loads[3].wait()
    masks = tap_masks(576)
    rows = []
    for b in range(3):
        w_b = jnp.concatenate([win_ref[(a * 3 + b) * 24 : (a * 3 + b) * 24 + 24, :].astype(F32) for a in range(3)], axis=0)
        rows.append(jnp.dot(w_b.T.astype(BF16), unfold(72), preferred_element_type=F32))
    for block in range(4):
        part = [row[8 * block : 8 * block + 8] for row in rows]
        a_in[64 * block : 64 * block + 64, :] = circulant(part, masks).astype(BF16)

    for copy in loads[4:]:
        copy.wait()

    def spread(o, carry):
        at = pl.ds(pl.multiple_of(o * 8, 8), 8)
        for i, value in enumerate((
            bin_ref[o] + emb_ref[0, o], gin_ref[o], sin_ref[o], bmid_ref[o], gmid_ref[o], smid_ref[o],
        )):
            splat[i, at, :] = jnp.full((8, NX), value, F32)
        return carry

    lax.fori_loop(0, FT, spread, 0)
    for o in range(CH):
        splat_out[8 * o : 8 * o + 8, :] = jnp.full((8, NX), bout_ref[o], F32)
    step, noise_scale = step_ref[0], nsc_ref[0]

    pl.semaphore_wait(barrier, 2 * (SIDE - 1))

    def send(src, dst, ss, rs, device):
        copy = pltpu.make_async_remote_copy(
            src_ref=src, dst_ref=dst, send_sem=ss, recv_sem=rs, device_id=device, device_id_type=MESH
        )
        copy.start()
        pending.append(copy)
        return copy

    def lanes(first, count=1):
        return slice(NX * first, NX * (first + count))

    sub = lax.broadcasted_iota(jnp.int32, (8, NX), 0)
    low = lax.broadcasted_iota(jnp.int32, (8, NX), 1) < NX // 2

    def lane_sums(groups):
        rows = jnp.concatenate([jnp.sum(t, axis=0, keepdims=True) for t in groups], axis=0)
        return jnp.broadcast_to(jnp.sum(rows, axis=1, keepdims=True), (8, NX))

    def fold(ref, planes, centre=None):
        plain, squares = [], []
        for gr in range(GR):
            tiles = []
            for q in planes:
                for c in range(4):
                    tile = ref[32 * gr + 8 * c : 32 * gr + 8 * c + 8, lanes(q)]
                    tiles.append(tile if centre is None else tile - jnp.broadcast_to(centre[gr : gr + 1], (8, NX)))
            plain.append(functools.reduce(lambda x, y: x + y, tiles))
            if centre is not None:
                squares.append(functools.reduce(lambda x, y: x + y, [t * t for t in tiles]))
        return plain, squares

    def centre_of(ref, planes):
        return lane_sums(fold(ref, planes)[0]) * (1.0 / (len(planes) * 4 * NY * NX))

    def announce(ref, inner, outer, centre, turn):
        plain, squares = fold(ref, inner, centre)
        plain2, squares2 = fold(ref, outer, centre)
        first = lane_sums([x + y for x, y in zip(plain, plain2)])
        second = lane_sums([x + y for x, y in zip(squares, squares2)])
        off = first * (1.0 / CELLS)
        tile = jnp.where(low, centre + off, second - first * off)
        stat[turn] = tile
        recv[turn, g] = tile
        return [
            send(stat.at[turn], recv.at[turn, g], stat_ss.at[turn, i], stat_rs.at[turn, i], {"gz": peer})
            for i, peer in enumerate(gz_peers)
        ]

    def gathered(copies, turn):
        for copy in copies:
            copy.wait_recv()
        every = recv[turn]
        total = jnp.sum(every, axis=0)
        mean = total * (1.0 / SIDE)
        off = every - mean[None]
        spread_of = jnp.sum(off * off, axis=0)
        var = (pltpu.roll(total, NX // 2, 1) + spread_of * CELLS) * (1.0 / (CELLS * SIDE))
        inv = lax.rsqrt(var + 1e-05)
        return jnp.where(low, mean, pltpu.roll(mean, NX // 2, 1)), jnp.where(low, inv, pltpu.roll(inv, NX // 2, 1))

    def activate(src, dst, planes, mean, inv, gain, shift):
        for gr in range(GR):
            at = slice(32 * gr, 32 * gr + 32)
            m = jnp.broadcast_to(mean[gr : gr + 1], (32, NX))
            f = jnp.broadcast_to(inv[gr : gr + 1], (32, NX)) * splat[gain, at, :]
            s = splat[shift, at, :]
            for q in planes:
                value = (src[at, lanes(q)] - m) * f + s
                dst[at, lanes(q)] = (value / (1.0 + jnp.exp(-value))).astype(BF16)

    def stack(src, planes):
        return jnp.concatenate([jnp.concatenate([src[:, lanes(q + a)] for q in planes], axis=1) for a in range(3)], axis=0)

    def turned(sweep, planes):
        for e in planes:
            plane = vext[sweep, e].reshape(CH * NY, NX)
            wide = plane.astype(F32)
            shift_in[0:64, lanes(e)] = pltpu.roll(wide, 1, 1).astype(BF16)
            shift_in[64:128, lanes(e)] = plane
            shift_in[128:192, lanes(e)] = pltpu.roll(wide, NX - 1, 1).astype(BF16)

    def lift(planes):
        out = jnp.dot(a_in[...], stack(shift_in, planes), preferred_element_type=F32)
        for i, q in enumerate(planes):
            lifted[:, lanes(q)] = out[:, lanes(i)] + splat[0]

    def middle(planes):
        rhs = stack(act, planes)
        taps = jnp.dot(a_mid[...], rhs, preferred_element_type=F32)
        for i, r in enumerate(planes):
            summed[:, lanes(r)] = (
                pltpu.roll(taps[0:256, lanes(i)], 1, 1) + taps[256:512, lanes(i)]
                + pltpu.roll(taps[512:768, lanes(i)], NX - 1, 1) + splat[3] + lifted[:, lanes(r + 1)]
            )

    for sweep in range(2):
        halo = [
            send(vext.at[sweep, pl.ds(NZ, HALO)], vext.at[sweep, pl.ds(0, HALO)],
                 halo_ss.at[sweep, 0], halo_rs.at[sweep, 0], {"gz": up}),
            send(vext.at[sweep, pl.ds(HALO, HALO)], vext.at[sweep, pl.ds(HALO + NZ, HALO)],
                 halo_ss.at[sweep, 1], halo_rs.at[sweep, 1], {"gz": down}),
        ]
        turned(sweep, (3, 4, 5, 6))
        lift((3, 4))
        centre = centre_of(lifted, (3, 4))
        for copy in halo:
            copy.wait_recv()
        turned(sweep, (2, 7))
        lift((2, 5))
        copies = announce(lifted, (3, 4), (2, 5), centre, 2 * sweep)
        turned(sweep, (0, 1, 8, 9))
        lift((0, 1, 6, 7))
        mean, inv = gathered(copies, 2 * sweep)

        activate(lifted, act, (1, 2, 3, 4, 5, 6), mean, inv, 1, 2)
        middle((2, 3))
        centre = centre_of(summed, (2, 3))
        middle((1, 4))
        copies = announce(summed, (2, 3), (1, 4), centre, 2 * sweep + 1)
        activate(lifted, act, (0, 7), mean, inv, 1, 2)
        middle((0, 5))
        mean, inv = gathered(copies, 2 * sweep + 1)

        activate(summed, actb, range(6), mean, inv, 4, 5)
        taps = jnp.dot(a_out[...], stack(actb, range(NZ)), preferred_element_type=F32)
        for z in range(NZ):
            predicted = (
                pltpu.roll(taps[0:64, lanes(z)], 1, 1) + taps[64:128, lanes(z)]
                + pltpu.roll(taps[128:192, lanes(z)], NX - 1, 1) + splat_out[...]
            )
            draws = noise_ref[:, z].astype(F32).reshape(CH * NY, NX)
            send1[sweep, 4 * z : 4 * z + 4] = (step * predicted + noise_scale * draws).reshape(4, 2, NY, NX)

        chunk_a[sweep, k] = send1[sweep, k]
        copies = [
            send(send1.at[sweep, peer], chunk_a.at[sweep, k], p1_ss.at[sweep, i], p1_rs.at[sweep, i], {"tm": peer})
            for i, peer in enumerate(tm_peers)
        ]
        for copy in copies:
            copy.wait_recv()
        state = lat_chunk[k]
        for s in range(SIDE):
            if sweep == 0:
                chunk_b[s] = state.reshape(16, NX).astype(BF16)
            state = state + chunk_a[sweep, s]
            if sweep == 1:
                send1[2, s] = state
        copies = []
        for i, peer in enumerate(tm_peers):
            if sweep == 0:
                src, dst = chunk_b.at[peer], vext.at[1, HALO + my_z, my_p]
            else:
                src, dst = send1.at[2, peer], out_ref.at[pl.ds(2 * my_p, 2), my_z]
            copies.append(send(src, dst, p2_ss.at[sweep, i], p2_rs.at[sweep, i], {"tm": peer}))
        if sweep == 0:
            vext[1, HALO + my_z, my_p] = chunk_b[k]
        else:
            out_ref[pl.ds(2 * my_p, 2), my_z] = send1[2, k]
        for copy in copies:
            copy.wait_recv()

    for copy in pending:
        copy.wait_send()


def shards(
    latent_start, noise_draws, time_embed, step_scale, noise_scale, w_in, b_in, gain_in, shift_in,
    w_mid, b_mid, gain_mid, shift_mid, w_out, b_out,
):
    vmem = pl.BlockSpec(memory_space=pltpu.VMEM)
    params = [pltpu.SMEM((FT,), F32)] * 6
    dma = pltpu.SemaphoreType.DMA
    out = pl.pallas_call(
        kernel,
        out_shape=pltpu.VMEM((CH, NZ, NY, NX), F32),
        in_specs=[pl.BlockSpec(memory_space=pltpu.HBM)] * 15,
        out_specs=vmem,
        scratch_shapes=[
            pltpu.VMEM((CH, NZ, NY, NX), F32), pltpu.VMEM((CH, NZ, NY, NX), BF16),
            pltpu.VMEM((27 * CH, FT), BF16), pltpu.VMEM((27 * FT, FT), BF16), pltpu.VMEM((27 * CH, FT), BF16),
            pltpu.SMEM((1, FT), F32), pltpu.SMEM((1,), F32), pltpu.SMEM((1,), F32), *params, pltpu.SMEM((CH,), F32),
            pltpu.VMEM((2, NZ + 2 * HALO, 4, 16, NX), BF16),
            pltpu.VMEM((192, (NZ + 2 * HALO) * NX), BF16),
            pltpu.VMEM((256, 8 * NX), F32),
            pltpu.VMEM((256, 8 * NX), BF16),
            pltpu.VMEM((256, 6 * NX), F32),
            pltpu.VMEM((256, 6 * NX), BF16),
            pltpu.VMEM((256, 576), BF16),
            pltpu.VMEM((768, 768), BF16),
            pltpu.VMEM((192, 768), BF16),
            pltpu.VMEM((864, 256), F32),
            pltpu.VMEM((6, 256, NX), F32),
            pltpu.VMEM((64, NX), F32),
            pltpu.VMEM((4, 8, NX), F32),
            pltpu.VMEM((4, SIDE, 8, NX), F32),
            pltpu.VMEM((3, SIDE, 2, NY, NX), F32),
            pltpu.VMEM((SIDE, 2, NY, NX), F32),
            pltpu.VMEM((2, SIDE, 2, NY, NX), F32),
            pltpu.VMEM((SIDE, 16, NX), BF16),
            dma((15,)), dma((2, 2)), dma((2, 2)), dma((4, SIDE)), dma((4, SIDE)),
            dma((2, SIDE)), dma((2, SIDE)), dma((2, SIDE)), dma((2, SIDE)),
        ],
        compiler_params=pltpu.CompilerParams(
            collective_id=0, has_side_effects=True, vmem_limit_bytes=60 * 2**20
        ),
    )(
        latent_start, noise_draws[0], time_embed, step_scale, noise_scale,
        w_in.transpose(2, 3, 4, 1, 0).reshape(27 * CH, FT), b_in, gain_in, shift_in,
        w_mid.transpose(2, 3, 4, 0, 1).reshape(27 * FT, FT), b_mid, gain_mid, shift_mid,
        w_out.transpose(2, 3, 4, 0, 1).reshape(27 * CH, FT), b_out,
    )
    return out[None]


def solution(mesh):
    in_specs = (
        P(None, "gz", None, None), P("tm", None, "gz", None, None), P("tm", None), P("tm"), P("tm"),
        P(), P(), P(), P(), P(), P(), P(), P(), P(), P(),
    )
    out_specs = P("tm", None, "gz", None, None)
    return jax.shard_map(shards, mesh=mesh, in_specs=in_specs, out_specs=out_specs, check_vma=False)
```

time: 76.3 us -> 66.5 us (0.87)
  local copies, waits for them, and re-layouts: 5.66 us -> 0.66 us
  Pallas kernels: 68.6 us -> 64.2 us
    unnamed x27 -> x1, local copies, waits for them, and re-layouts: 5.66 us -> 0.66 us
    pallas_call x1, Pallas kernels: 68.6 us -> 64.2 us  [shards(): pl.pallas_call(kernel, out_shape=pltpu.VMEM((CH, NZ, NY, NX), F32), in_sp...]
where the time goes in v2:
time: 66.5 us; the launch traced here: 66.1 us
  Pallas kernels  64.2 us (97%)
  between operations  1.3 us (2%)
    pallas_call x1, Pallas kernels, shards(): pl.pallas_call(kernel, out_shape=pltpu.VMEM((CH, NZ, NY, NX), F32), in_sp...  64.2 us

profile of v2, /device:TPU:1, one launch (start us, length us, event | category | flops | bytes accessed | tf_op | source)
XLA Modules:
  0.0 66.1 jit_solution(12960711611864454395)
XLA Ops:
  1.3 64.2 %shard_map.145 = f32[8,4,8,128]{3,2,1,0:T(8,128)S(1)} custom-call(f32[8,4,8,128]{3,2,1,0:T(8,128)} %lat_hbm.1, bf16[8,4,8,128]{3,2,1,0:T(8,128)(2,1)} %bitcast.13, f32[1,32]{1,0:T(1,128)} %emb_hbm.1, f32[1]{0:T(128)S(6)} %copy.18.step_hbm, f32[1]{0:T(128)S(6)} %copy.19.nsc_hbm, bf16[216,32]{1,0:T(8,128)(2,1)} %bitcast.14, f32[32]{0:T(128)} %bin_hbm.1, ...), custom_call_target="tpu_custom_call" | custom-call | tf_op jit(solution)/shard_map/pallas_call | solution.py:312
  65.5 0.7 copy.17

commit v3 on v2

--- a/solution.py
+++ b/solution.py
@@ -63,9 +63,9 @@
     out_ref,
     lat_ref, noise_ref, win_ref, wmid_ref, wout_ref, emb_ref, step_ref, nsc_ref,
     bin_ref, gin_ref, sin_ref, bmid_ref, gmid_ref, smid_ref, bout_ref,
-    vext, shift_in, lifted, act, summed, actb, a_in, a_mid, a_out, x_mid, splat, splat_out,
+    vext, shift_in, lifted, act, summed, actb, a_in, a_mid, a_out, x_mid, splat, splat_out, drift,
     stat, recv, send1, lat_chunk, chunk_a, chunk_b,
-    load_sem, halo_ss, halo_rs, stat_ss, stat_rs, p1_ss, p1_rs, p2_ss, p2_rs,
+    relay_sem, load_sem, halo_ss, halo_rs, edge_ss, edge_rs, stat_ss, stat_rs, p1_ss, p1_rs, p2_ss, p2_rs,
 ):
     k = lax.axis_index("tm")
     g = lax.axis_index("gz")
@@ -76,7 +76,10 @@
     pending = []
 
     barrier = pltpu.get_barrier_semaphore()
-    for peer in tm_peers:
+    beside = [shifted(k, 1, 0), shifted(k, SIDE // 2 - 1, 0)]
+    beyond = [shifted(k, 2, 0), shifted(k, SIDE // 2 - 2, 0)]
+    across = [shifted(k, 0, 1)]
+    for peer in beside + across:
         pl.semaphore_signal(barrier, inc=1, device_id={"tm": peer}, device_id_type=MESH)
     for peer in gz_peers:
         pl.semaphore_signal(barrier, inc=1, device_id={"gz": peer}, device_id_type=MESH)
@@ -97,18 +100,24 @@
         vext[0, HALO + z] = plane.reshape(4, 16, NX).astype(BF16)
         lat_chunk[4 * z : 4 * z + 4] = plane.reshape(4, 2, NY, NX)
 
-    loads[1].wait()
-    x_mid[...] = jnp.dot(wmid_ref[...], unfold(FT), preferred_element_type=F32)
-    masks = tap_masks(256)
-    for a in range(3):
-        for block in range(12):
-            rows = [x_mid[(a * 3 + b) * 96 + 8 * block : (a * 3 + b) * 96 + 8 * block + 8, :] for b in range(3)]
-            a_mid[64 * block : 64 * block + 64, 256 * a : 256 * a + 256] = circulant(rows, masks).astype(BF16)
-    loads[2].wait()
-    x_out = jnp.dot(wout_ref[...], unfold(FT), preferred_element_type=F32)
-    for a in range(3):
-        rows = [x_out[(a * 3 + b) * 24 : (a * 3 + b) * 24 + 24] for b in range(3)]
-        a_out[:, 256 * a : 256 * a + 256] = circulant(rows, masks).astype(BF16)
+    def load_mid():
+        loads[1].wait()
+        x_mid[...] = jnp.dot(wmid_ref[...], unfold(FT), preferred_element_type=F32)
+        masks = tap_masks(256)
+        for a in range(3):
+            for block in range(12):
+                first = a * 288 + 8 * block
+                rows = [x_mid[first + 96 * b : first + 96 * b + 8, :] for b in range(3)]
+                a_mid[64 * block : 64 * block + 64, 256 * a : 256 * a + 256] = circulant(rows, masks).astype(BF16)
+
+    def load_out():
+        loads[2].wait()
+        masks = tap_masks(256)
+        x_out = jnp.dot(wout_ref[...], unfold(FT), preferred_element_type=F32)
+        for a in range(3):
+            rows = [x_out[(a * 3 + b) * 24 : (a * 3 + b) * 24 + 24] for b in range(3)]
+            a_out[:, 256 * a : 256 * a + 256] = circulant(rows, masks).astype(BF16)
+
     loads[3].wait()
     masks = tap_masks(576)
     rows = []
@@ -125,7 +134,8 @@
     def spread(o, carry):
         at = pl.ds(pl.multiple_of(o * 8, 8), 8)
         for i, value in enumerate((
-            bin_ref[o] + emb_ref[0, o], gin_ref[o], sin_ref[o], bmid_ref[o], gmid_ref[o], smid_ref[o],
+            bin_ref[o] + emb_ref[0, o], 0.5 * gin_ref[o], 0.5 * sin_ref[o],
+            bmid_ref[o], 0.5 * gmid_ref[o], 0.5 * smid_ref[o],
         )):
             splat[i, at, :] = jnp.full((8, NX), value, F32)
         return carry
@@ -135,7 +145,13 @@
         splat_out[8 * o : 8 * o + 8, :] = jnp.full((8, NX), bout_ref[o], F32)
     step, noise_scale = step_ref[0], nsc_ref[0]
 
-    pl.semaphore_wait(barrier, 2 * (SIDE - 1))
+    pl.semaphore_wait(barrier, len(GZ_ORDER) + len(beside + across))
+
+    def relay(turn, peers):
+        for peer in peers:
+            pl.semaphore_signal(relay_sem.at[turn], inc=1, device_id={"tm": peer}, device_id_type=MESH)
+
+    relay(0, beside)
 
     def send(src, dst, ss, rs, device):
         copy = pltpu.make_async_remote_copy(
@@ -144,6 +160,15 @@
         copy.start()
         pending.append(copy)
         return copy
+
+    def settle(copies):
+        fresh = {id(copy) for copy in copies}
+        for copy in pending:
+            if id(copy) not in fresh:
+                copy.wait_send()
+        pending[:] = copies
+        for copy in copies:
+            copy.wait_recv()
 
     def lanes(first, count=1):
         return slice(NX * first, NX * (first + count))
@@ -186,8 +211,7 @@
         ]
 
     def gathered(copies, turn):
-        for copy in copies:
-            copy.wait_recv()
+        settle(copies)
         every = recv[turn]
         total = jnp.sum(every, axis=0)
         mean = total * (1.0 / SIDE)
@@ -204,8 +228,8 @@
             f = jnp.broadcast_to(inv[gr : gr + 1], (32, NX)) * splat[gain, at, :]
             s = splat[shift, at, :]
             for q in planes:
-                value = (src[at, lanes(q)] - m) * f + s
-                dst[at, lanes(q)] = (value / (1.0 + jnp.exp(-value))).astype(BF16)
+                half = (src[at, lanes(q)] - m) * f + s
+                dst[at, lanes(q)] = (half + half * jnp.tanh(half)).astype(BF16)
 
     def stack(src, planes):
         return jnp.concatenate([jnp.concatenate([src[:, lanes(q + a)] for q in planes], axis=1) for a in range(3)], axis=0)
@@ -233,23 +257,47 @@
             )
 
     for sweep in range(2):
-        halo = [
-            send(vext.at[sweep, pl.ds(NZ, HALO)], vext.at[sweep, pl.ds(0, HALO)],
-                 halo_ss.at[sweep, 0], halo_rs.at[sweep, 0], {"gz": up}),
-            send(vext.at[sweep, pl.ds(HALO, HALO)], vext.at[sweep, pl.ds(HALO + NZ, HALO)],
-                 halo_ss.at[sweep, 1], halo_rs.at[sweep, 1], {"gz": down}),
-        ]
-        turned(sweep, (3, 4, 5, 6))
-        lift((3, 4))
-        centre = centre_of(lifted, (3, 4))
-        for copy in halo:
-            copy.wait_recv()
-        turned(sweep, (2, 7))
-        lift((2, 5))
-        copies = announce(lifted, (3, 4), (2, 5), centre, 2 * sweep)
-        turned(sweep, (0, 1, 8, 9))
-        lift((0, 1, 6, 7))
+        if sweep == 0:
+            halo = [
+                send(vext.at[0, pl.ds(NZ, HALO)], vext.at[0, pl.ds(0, HALO)],
+                     halo_ss.at[0, 0], halo_rs.at[0, 0], {"gz": up}),
+                send(vext.at[0, pl.ds(HALO, HALO)], vext.at[0, pl.ds(HALO + NZ, HALO)],
+                     halo_ss.at[0, 1], halo_rs.at[0, 1], {"gz": down}),
+            ]
+            for z in range(NZ):
+                draws = noise_ref[:, z].astype(F32).reshape(CH * NY, NX)
+                drift[z] = step * splat_out[...] + noise_scale * draws
+            turned(sweep, (3, 4, 5, 6))
+            lift((3, 4))
+            centre = centre_of(lifted, (3, 4))
+            settle(halo)
+            turned(sweep, (2, 7))
+            lift((2, 5))
+            copies = announce(lifted, (3, 4), (2, 5), centre, 0)
+            pl.semaphore_wait(relay_sem.at[0], 2)
+            relay(1, beyond)
+            turned(sweep, (0, 1, 8, 9))
+            lift((0, 1, 6, 7))
+            load_mid()
+        else:
+            halo = [
+                send(vext.at[1, pl.ds(NZ, 2)], vext.at[1, pl.ds(0, 2)],
+                     halo_ss.at[1, 0], halo_rs.at[1, 0], {"gz": up}),
+                send(vext.at[1, pl.ds(NZ, 2)], vext.at[1, pl.ds(HALO + NZ + 1, 2)],
+                     halo_ss.at[1, 1], halo_rs.at[1, 1], {"gz": down}),
+            ]
+            turned(sweep, (2, 3, 4, 5, 6, 7))
+            lift((2, 3, 4, 5))
+            centre = centre_of(lifted, (3, 4))
+            copies = announce(lifted, (3, 4), (2, 5), centre, 2)
+            for copy in halo:
+                copy.wait_recv()
+            turned(sweep, (0, 1, 8, 9))
+            lift((0, 1, 6, 7))
         mean, inv = gathered(copies, 2 * sweep)
+        if sweep == 0:
+            pl.semaphore_wait(relay_sem.at[1], 2)
+            relay(2, across)
 
         activate(lifted, act, (1, 2, 3, 4, 5, 6), mean, inv, 1, 2)
         middle((2, 3))
@@ -258,6 +306,9 @@
         copies = announce(summed, (2, 3), (1, 4), centre, 2 * sweep + 1)
         activate(lifted, act, (0, 7), mean, inv, 1, 2)
         middle((0, 5))
+        if sweep == 0:
+            load_out()
+            pl.semaphore_wait(relay_sem.at[2], 1)
         mean, inv = gathered(copies, 2 * sweep + 1)
 
         activate(summed, actb, range(6), mean, inv, 4, 5)
@@ -265,18 +316,16 @@
         for z in range(NZ):
             predicted = (
                 pltpu.roll(taps[0:64, lanes(z)], 1, 1) + taps[64:128, lanes(z)]
-                + pltpu.roll(taps[128:192, lanes(z)], NX - 1, 1) + splat_out[...]
+                + pltpu.roll(taps[128:192, lanes(z)], NX - 1, 1)
             )
-            draws = noise_ref[:, z].astype(F32).reshape(CH * NY, NX)
-            send1[sweep, 4 * z : 4 * z + 4] = (step * predicted + noise_scale * draws).reshape(4, 2, NY, NX)
+            send1[sweep, 4 * z : 4 * z + 4] = (step * predicted + drift[z]).reshape(4, 2, NY, NX)
 
         chunk_a[sweep, k] = send1[sweep, k]
         copies = [
             send(send1.at[sweep, peer], chunk_a.at[sweep, k], p1_ss.at[sweep, i], p1_rs.at[sweep, i], {"tm": peer})
             for i, peer in enumerate(tm_peers)
         ]
-        for copy in copies:
-            copy.wait_recv()
+        settle(copies)
         state = lat_chunk[k]
         for s in range(SIDE):
             if sweep == 0:
@@ -285,6 +334,23 @@
             if sweep == 1:
                 send1[2, s] = state
         copies = []
+        if sweep == 0:
+            face = (my_z == 0) | (my_z == NZ - 1)
+            first = my_z == 0
+            other, plane = jnp.where(first, down, up), jnp.where(first, HALO + NZ, HALO - 1)
+            edge = jnp.where(first, 4, 0) + my_p
+
+            def edge_copy(i, peer):
+                return pltpu.make_async_remote_copy(
+                    src_ref=chunk_b.at[peer], dst_ref=vext.at[1, plane, my_p], send_sem=edge_ss.at[i],
+                    recv_sem=edge_rs.at[edge], device_id={"tm": peer, "gz": other}, device_id_type=MESH,
+                )
+
+            @pl.when(face)
+            def _():
+                for i, peer in enumerate(tm_peers + [k]):
+                    edge_copy(i, peer).start()
+
         for i, peer in enumerate(tm_peers):
             if sweep == 0:
                 src, dst = chunk_b.at[peer], vext.at[1, HALO + my_z, my_p]
@@ -295,8 +361,18 @@
             vext[1, HALO + my_z, my_p] = chunk_b[k]
         else:
             out_ref[pl.ds(2 * my_p, 2), my_z] = send1[2, k]
-        for copy in copies:
-            copy.wait_recv()
+        settle(copies)
+        if sweep == 0:
+            for i in range(8):
+                pltpu.make_async_remote_copy(
+                    src_ref=chunk_b.at[0], dst_ref=vext.at[1, HALO + NZ if i >= 4 else HALO - 1, i % 4],
+                    send_sem=edge_ss.at[0], recv_sem=edge_rs.at[i], device_id={"gz": up}, device_id_type=MESH,
+                ).wait_recv()
+
+            @pl.when(face)
+            def _():
+                for i, peer in enumerate(tm_peers + [k]):
+                    edge_copy(i, peer).wait_send()
 
     for copy in pending:
         copy.wait_send()
@@ -330,13 +406,14 @@
             pltpu.VMEM((864, 256), F32),
             pltpu.VMEM((6, 256, NX), F32),
             pltpu.VMEM((64, NX), F32),
+            pltpu.VMEM((NZ, 64, NX), F32),
             pltpu.VMEM((4, 8, NX), F32),
             pltpu.VMEM((4, SIDE, 8, NX), F32),
             pltpu.VMEM((3, SIDE, 2, NY, NX), F32),
             pltpu.VMEM((SIDE, 2, NY, NX), F32),
             pltpu.VMEM((2, SIDE, 2, NY, NX), F32),
             pltpu.VMEM((SIDE, 16, NX), BF16),
-            dma((15,)), dma((2, 2)), dma((2, 2)), dma((4, SIDE)), dma((4, SIDE)),
+            pltpu.SemaphoreType.REGULAR((3,)), dma((15,)), dma((2, 2)), dma((2, 2)), dma((SIDE,)), dma((8,)), dma((4, SIDE)), dma((4, SIDE)),
             dma((2, SIDE)), dma((2, SIDE)), dma((2, SIDE)), dma((2, SIDE)),
         ],
         compiler_params=pltpu.CompilerParams(

time: 66.5 us -> 61.9 us (0.931)
  Pallas kernels: 64.2 us -> 59.8 us
    pallas_call x1, Pallas kernels: 64.2 us -> 59.8 us  [shards(): pl.pallas_call(kernel, out_shape=pltpu.VMEM((CH, NZ, NY, NX), F32), in_sp...]
where the time goes in v3:
time: 61.9 us; the launch traced here: 61.7 us
  Pallas kernels  59.8 us (97%)
  between operations  1.3 us (2%)
  local copies, waits for them, and re-layouts  0.66 us (1%)
    pallas_call x1, Pallas kernels, shards(): pl.pallas_call(kernel, out_shape=pltpu.VMEM((CH, NZ, NY, NX), F32), in_sp...  59.8 us

profile of v3, /device:TPU:1, one launch (start us, length us, event | category | flops | bytes accessed | tf_op | source)
XLA Modules:
  0.0 61.7 jit_solution(11924282408432601961)
XLA Ops:
  1.3 59.8 %shard_map.145 = f32[8,4,8,128]{3,2,1,0:T(8,128)S(1)} custom-call(f32[8,4,8,128]{3,2,1,0:T(8,128)} %lat_hbm.1, bf16[8,4,8,128]{3,2,1,0:T(8,128)(2,1)} %bitcast.13, f32[1,32]{1,0:T(1,128)} %emb_hbm.1, f32[1]{0:T(128)S(6)} %copy.18.step_hbm, f32[1]{0:T(128)S(6)} %copy.19.nsc_hbm, bf16[216,32]{1,0:T(8,128)(2,1)} %bitcast.14, f32[32]{0:T(128)} %bin_hbm.1, ...), custom_call_target="tpu_custom_call" | custom-call | tf_op jit(solution)/shard_map/pallas_call | solution.py:388
  61.1 0.7 %copy.17 = f32[1,8,4,8,128]{4,3,2,1,0:T(8,128)} copy(f32[1,8,4,8,128]{4,3,2,1,0:T(8,128)S(1)} %bitcast.11) | data formatting | bytes 262144

commit v4 on v3

--- a/solution.py
+++ b/solution.py
@@ -16,10 +16,8 @@
 CELLS = (FT // GR) * NZ * NY * NX
 
 GZ_ORDER = (12, 13, 4, 5, 8, 9, 14, 15, 10, 11, 2, 3, 6, 7, 1)
-TM_ORDER = (
-    (4, 1), (3, 1), (5, 1), (4, 0), (2, 1), (6, 1), (3, 0), (5, 0),
-    (1, 1), (7, 1), (2, 0), (6, 0), (0, 1), (1, 0), (7, 0),
-)
+HALF = 8
+HALF_ORDER = (7, 5, 6, 3, 4, 1, 2)
 
 
 def flip(place, bits):
@@ -27,13 +25,6 @@
         if bits & bit:
             place = place + bit - 2 * bit * lax.rem(lax.div(place, bit), 2)
     return place
-
-
-def shifted(place, steps, other):
-    z, half = lax.div(place, 2), lax.rem(place, 2)
-    if other:
-        half = 1 - half
-    return 2 * lax.rem(z + steps, SIDE // 2) + half
 
 
 def unfold(count):
@@ -64,25 +55,29 @@
     lat_ref, noise_ref, win_ref, wmid_ref, wout_ref, emb_ref, step_ref, nsc_ref,
     bin_ref, gin_ref, sin_ref, bmid_ref, gmid_ref, smid_ref, bout_ref,
     vext, shift_in, lifted, act, summed, actb, a_in, a_mid, a_out, x_mid, splat, splat_out, drift,
-    stat, recv, send1, lat_chunk, chunk_a, chunk_b,
-    relay_sem, load_sem, halo_ss, halo_rs, edge_ss, edge_rs, stat_ss, stat_rs, p1_ss, p1_rs, p2_ss, p2_rs,
+    stat, recv, send1, lat_chunk, chunk_a, chunk_b, half_sum, earlier_sum,
+    relay_sem, load_sem, halo_ss, halo_rs, edge_ss, edge_rs, stat_ss, stat_rs, p1_ss, p1_rs, p2_ss, p2_rs, sum_ss, sum_rs,
 ):
     k = lax.axis_index("tm")
     g = lax.axis_index("gz")
     up, down = lax.rem(g + 1, SIDE), lax.rem(g + SIDE - 1, SIDE)
     gz_peers = [flip(g, bits) for bits in GZ_ORDER]
-    tm_peers = [shifted(k, steps, other) for steps, other in TM_ORDER]
-    my_z, my_p = lax.div(k, 4), lax.rem(k, 4)
+    tm_peers = [flip(k, bits) for bits in HALF_ORDER]
+    late, place = lax.div(k, HALF), lax.rem(k, HALF)
+    twin = flip(k, HALF)
+    my_z, my_p = lax.div(place, 2), lax.rem(place, 2)
     pending = []
 
     barrier = pltpu.get_barrier_semaphore()
-    beside = [shifted(k, 1, 0), shifted(k, SIDE // 2 - 1, 0)]
-    beyond = [shifted(k, 2, 0), shifted(k, SIDE // 2 - 2, 0)]
-    across = [shifted(k, 0, 1)]
+    beside, across = [flip(k, 2), flip(k, 4)], [flip(k, 1)]
     for peer in beside + across:
         pl.semaphore_signal(barrier, inc=1, device_id={"tm": peer}, device_id_type=MESH)
     for peer in gz_peers:
         pl.semaphore_signal(barrier, inc=1, device_id={"gz": peer}, device_id_type=MESH)
+
+    @pl.when(late == 0)
+    def _():
+        pl.semaphore_signal(barrier, inc=1, device_id={"tm": twin}, device_id_type=MESH)
 
     loads = []
     for src, dst in (
@@ -98,7 +93,47 @@
     for z in range(NZ):
         plane = lat_ref[:, z].reshape(CH * NY, NX)
         vext[0, HALO + z] = plane.reshape(4, 16, NX).astype(BF16)
-        lat_chunk[4 * z : 4 * z + 4] = plane.reshape(4, 2, NY, NX)
+        lat_chunk[2 * z : 2 * z + 2] = plane.reshape(2, 4, NY, NX)
+
+    pl.semaphore_wait(barrier, len(GZ_ORDER) + len(beside + across) + late)
+
+    def relay(turn, peers):
+        for peer in peers:
+            pl.semaphore_signal(relay_sem.at[turn], inc=1, device_id={"tm": peer}, device_id_type=MESH)
+
+    relay(0, beside)
+
+    @pl.when(late == 1)
+    def _():
+        relay(2, [twin])
+
+    @pl.when(late == 0)
+    def _():
+        earlier_sum[...] = jnp.zeros_like(earlier_sum)
+
+    def send(src, dst, ss, rs, device):
+        copy = pltpu.make_async_remote_copy(
+            src_ref=src, dst_ref=dst, send_sem=ss, recv_sem=rs, device_id=device, device_id_type=MESH
+        )
+        copy.start()
+        pending.append(copy)
+        return copy
+
+    def settle(copies):
+        fresh = {id(copy) for copy in copies}
+        for copy in pending:
+            if id(copy) not in fresh:
+                copy.wait_send()
+        pending[:] = copies
+        for copy in copies:
+            copy.wait_recv()
+
+    halo = [
+        send(vext.at[0, pl.ds(NZ, HALO)], vext.at[0, pl.ds(0, HALO)],
+             halo_ss.at[0, 0], halo_rs.at[0, 0], {"gz": up}),
+        send(vext.at[0, pl.ds(HALO, HALO)], vext.at[0, pl.ds(HALO + NZ, HALO)],
+             halo_ss.at[0, 1], halo_rs.at[0, 1], {"gz": down}),
+    ]
 
     def load_mid():
         loads[1].wait()
@@ -144,31 +179,6 @@
     for o in range(CH):
         splat_out[8 * o : 8 * o + 8, :] = jnp.full((8, NX), bout_ref[o], F32)
     step, noise_scale = step_ref[0], nsc_ref[0]
-
-    pl.semaphore_wait(barrier, len(GZ_ORDER) + len(beside + across))
-
-    def relay(turn, peers):
-        for peer in peers:
-            pl.semaphore_signal(relay_sem.at[turn], inc=1, device_id={"tm": peer}, device_id_type=MESH)
-
-    relay(0, beside)
-
-    def send(src, dst, ss, rs, device):
-        copy = pltpu.make_async_remote_copy(
-            src_ref=src, dst_ref=dst, send_sem=ss, recv_sem=rs, device_id=device, device_id_type=MESH
-        )
-        copy.start()
-        pending.append(copy)
-        return copy
-
-    def settle(copies):
-        fresh = {id(copy) for copy in copies}
-        for copy in pending:
-            if id(copy) not in fresh:
-                copy.wait_send()
-        pending[:] = copies
-        for copy in copies:
-            copy.wait_recv()
 
     def lanes(first, count=1):
         return slice(NX * first, NX * (first + count))
@@ -258,12 +268,6 @@
 
     for sweep in range(2):
         if sweep == 0:
-            halo = [
-                send(vext.at[0, pl.ds(NZ, HALO)], vext.at[0, pl.ds(0, HALO)],
-                     halo_ss.at[0, 0], halo_rs.at[0, 0], {"gz": up}),
-                send(vext.at[0, pl.ds(HALO, HALO)], vext.at[0, pl.ds(HALO + NZ, HALO)],
-                     halo_ss.at[0, 1], halo_rs.at[0, 1], {"gz": down}),
-            ]
             for z in range(NZ):
                 draws = noise_ref[:, z].astype(F32).reshape(CH * NY, NX)
                 drift[z] = step * splat_out[...] + noise_scale * draws
@@ -275,7 +279,7 @@
             lift((2, 5))
             copies = announce(lifted, (3, 4), (2, 5), centre, 0)
             pl.semaphore_wait(relay_sem.at[0], 2)
-            relay(1, beyond)
+            relay(1, across)
             turned(sweep, (0, 1, 8, 9))
             lift((0, 1, 6, 7))
             load_mid()
@@ -296,8 +300,7 @@
             lift((0, 1, 6, 7))
         mean, inv = gathered(copies, 2 * sweep)
         if sweep == 0:
-            pl.semaphore_wait(relay_sem.at[1], 2)
-            relay(2, across)
+            pl.semaphore_wait(relay_sem.at[1], 1)
 
         activate(lifted, act, (1, 2, 3, 4, 5, 6), mean, inv, 1, 2)
         middle((2, 3))
@@ -308,7 +311,6 @@
         middle((0, 5))
         if sweep == 0:
             load_out()
-            pl.semaphore_wait(relay_sem.at[2], 1)
         mean, inv = gathered(copies, 2 * sweep + 1)
 
         activate(summed, actb, range(6), mean, inv, 4, 5)
@@ -318,18 +320,37 @@
                 pltpu.roll(taps[0:64, lanes(z)], 1, 1) + taps[64:128, lanes(z)]
                 + pltpu.roll(taps[128:192, lanes(z)], NX - 1, 1)
             )
-            send1[sweep, 4 * z : 4 * z + 4] = (step * predicted + drift[z]).reshape(4, 2, NY, NX)
-
-        chunk_a[sweep, k] = send1[sweep, k]
+            send1[sweep, 2 * z : 2 * z + 2] = (step * predicted + drift[z]).reshape(2, 4, NY, NX)
+
+        chunk_a[sweep, place] = send1[sweep, place]
         copies = [
-            send(send1.at[sweep, peer], chunk_a.at[sweep, k], p1_ss.at[sweep, i], p1_rs.at[sweep, i], {"tm": peer})
+            send(send1.at[sweep, lax.rem(peer, HALF)], chunk_a.at[sweep, place],
+                 p1_ss.at[sweep, i], p1_rs.at[sweep, i], {"tm": peer})
             for i, peer in enumerate(tm_peers)
         ]
         settle(copies)
-        state = lat_chunk[k]
-        for s in range(SIDE):
+
+        def onward():
+            return pltpu.make_async_remote_copy(
+                src_ref=half_sum.at[sweep], dst_ref=earlier_sum.at[sweep], send_sem=sum_ss.at[sweep],
+                recv_sem=sum_rs.at[sweep], device_id={"tm": twin}, device_id_type=MESH,
+            )
+
+        @pl.when(late == 0)
+        def _():
+            half_sum[sweep] = jnp.sum(chunk_a[sweep], axis=0)
             if sweep == 0:
-                chunk_b[s] = state.reshape(16, NX).astype(BF16)
+                pl.semaphore_wait(relay_sem.at[2], 1)
+            onward().start()
+
+        @pl.when(late == 1)
+        def _():
+            onward().wait_recv()
+
+        state = lat_chunk[place] + earlier_sum[sweep]
+        for s in range(HALF):
+            if sweep == 0:
+                chunk_b[s] = state.reshape(2, 16, NX).astype(BF16)
             state = state + chunk_a[sweep, s]
             if sweep == 1:
                 send1[2, s] = state
@@ -338,12 +359,13 @@
             face = (my_z == 0) | (my_z == NZ - 1)
             first = my_z == 0
             other, plane = jnp.where(first, down, up), jnp.where(first, HALO + NZ, HALO - 1)
-            edge = jnp.where(first, 4, 0) + my_p
+            edge = jnp.where(first, 2, 0) + my_p
 
             def edge_copy(i, peer):
                 return pltpu.make_async_remote_copy(
-                    src_ref=chunk_b.at[peer], dst_ref=vext.at[1, plane, my_p], send_sem=edge_ss.at[i],
-                    recv_sem=edge_rs.at[edge], device_id={"tm": peer, "gz": other}, device_id_type=MESH,
+                    src_ref=chunk_b.at[lax.rem(peer, HALF)], dst_ref=vext.at[1, plane, pl.ds(2 * my_p, 2)],
+                    send_sem=edge_ss.at[i], recv_sem=edge_rs.at[edge],
+                    device_id={"tm": peer, "gz": other}, device_id_type=MESH,
                 )
 
             @pl.when(face)
@@ -353,19 +375,20 @@
 
         for i, peer in enumerate(tm_peers):
             if sweep == 0:
-                src, dst = chunk_b.at[peer], vext.at[1, HALO + my_z, my_p]
+                src, dst = chunk_b.at[lax.rem(peer, HALF)], vext.at[1, HALO + my_z, pl.ds(2 * my_p, 2)]
             else:
-                src, dst = send1.at[2, peer], out_ref.at[pl.ds(2 * my_p, 2), my_z]
+                src, dst = send1.at[2, lax.rem(peer, HALF)], out_ref.at[pl.ds(4 * my_p, 4), my_z]
             copies.append(send(src, dst, p2_ss.at[sweep, i], p2_rs.at[sweep, i], {"tm": peer}))
         if sweep == 0:
-            vext[1, HALO + my_z, my_p] = chunk_b[k]
+            vext[1, HALO + my_z, pl.ds(2 * my_p, 2)] = chunk_b[place]
         else:
-            out_ref[pl.ds(2 * my_p, 2), my_z] = send1[2, k]
+            out_ref[pl.ds(4 * my_p, 4), my_z] = send1[2, place]
         settle(copies)
         if sweep == 0:
-            for i in range(8):
+            for i in range(4):
                 pltpu.make_async_remote_copy(
-                    src_ref=chunk_b.at[0], dst_ref=vext.at[1, HALO + NZ if i >= 4 else HALO - 1, i % 4],
+                    src_ref=chunk_b.at[0],
+                    dst_ref=vext.at[1, HALO + NZ if i >= 2 else HALO - 1, pl.ds(2 * (i % 2), 2)],
                     send_sem=edge_ss.at[0], recv_sem=edge_rs.at[i], device_id={"gz": up}, device_id_type=MESH,
                 ).wait_recv()
 
@@ -373,6 +396,10 @@
             def _():
                 for i, peer in enumerate(tm_peers + [k]):
                     edge_copy(i, peer).wait_send()
+
+        @pl.when(late == 0)
+        def _():
+            onward().wait_send()
 
     for copy in pending:
         copy.wait_send()
@@ -388,7 +415,7 @@
     out = pl.pallas_call(
         kernel,
         out_shape=pltpu.VMEM((CH, NZ, NY, NX), F32),
-        in_specs=[pl.BlockSpec(memory_space=pltpu.HBM)] * 15,
+        in_specs=[pl.BlockSpec(memory_space=pl.ANY)] * 15,
         out_specs=vmem,
         scratch_shapes=[
             pltpu.VMEM((CH, NZ, NY, NX), F32), pltpu.VMEM((CH, NZ, NY, NX), BF16),
@@ -409,12 +436,14 @@
             pltpu.VMEM((NZ, 64, NX), F32),
             pltpu.VMEM((4, 8, NX), F32),
             pltpu.VMEM((4, SIDE, 8, NX), F32),
-            pltpu.VMEM((3, SIDE, 2, NY, NX), F32),
-            pltpu.VMEM((SIDE, 2, NY, NX), F32),
-            pltpu.VMEM((2, SIDE, 2, NY, NX), F32),
-            pltpu.VMEM((SIDE, 16, NX), BF16),
-            pltpu.SemaphoreType.REGULAR((3,)), dma((15,)), dma((2, 2)), dma((2, 2)), dma((SIDE,)), dma((8,)), dma((4, SIDE)), dma((4, SIDE)),
-            dma((2, SIDE)), dma((2, SIDE)), dma((2, SIDE)), dma((2, SIDE)),
+            pltpu.VMEM((3, HALF, 4, NY, NX), F32),
+            pltpu.VMEM((HALF, 4, NY, NX), F32),
+            pltpu.VMEM((2, HALF, 4, NY, NX), F32),
+            pltpu.VMEM((HALF, 2, 16, NX), BF16),
+            pltpu.VMEM((2, 4, NY, NX), F32),
+            pltpu.VMEM((2, 4, NY, NX), F32),
+            pltpu.SemaphoreType.REGULAR((3,)), dma((15,)), dma((2, 2)), dma((2, 2)), dma((HALF,)), dma((4,)), dma((4, SIDE)), dma((4, SIDE)),
+            dma((2, HALF)), dma((2, HALF)), dma((2, HALF)), dma((2, HALF)), dma((2,)), dma((2,)),
         ],
         compiler_params=pltpu.CompilerParams(
             collective_id=0, has_side_effects=True, vmem_limit_bytes=60 * 2**20

time: 61.9 us -> 56.7 us (0.916)
  the two profiles are of different devices: /device:TPU:1 before, /device:TPU:224 now
where the time goes in v4:
time: 56.7 us; the launch traced here: 56.6 us
  Pallas kernels  54.7 us (96%)
  between operations  1.3 us (2%)
  local copies, waits for them, and re-layouts  0.66 us (1%)
    pallas_call x1, Pallas kernels, shards(): pl.pallas_call(kernel, out_shape=pltpu.VMEM((CH, NZ, NY, NX), F32), in_sp...  54.7 us

profile of v4, /device:TPU:224, one launch (start us, length us, event | category | flops | bytes accessed | tf_op | source)
XLA Modules:
  0.0 56.6 jit_solution(4732010882743717651)
XLA Ops:
  1.3 54.7 %shard_map.145 = f32[8,4,8,128]{3,2,1,0:T(8,128)S(1)} custom-call(f32[8,4,8,128]{3,2,1,0:T(8,128)} %lat_hbm.1, bf16[8,4,8,128]{3,2,1,0:T(8,128)(2,1)} %bitcast.13, f32[1,32]{1,0:T(1,128)} %emb_hbm.1, f32[1]{0:T(128)S(6)} %copy.18.step_hbm, f32[1]{0:T(128)S(6)} %copy.19.nsc_hbm, bf16[216,32]{1,0:T(8,128)(2,1)} %bitcast.14, f32[32]{0:T(128)} %bin_hbm.1, ...), custom_call_target="tpu_custom_call" | custom-call | tf_op jit(solution)/shard_map/pallas_call | solution.py:415
  56.0 0.7 %copy.17 = f32[1,8,4,8,128]{4,3,2,1,0:T(8,128)} copy(f32[1,8,4,8,128]{4,3,2,1,0:T(8,128)S(1)} %bitcast.11) | data formatting | bytes 262144

commit v5 on v4

--- a/solution.py
+++ b/solution.py
@@ -64,15 +64,21 @@
     gz_peers = [flip(g, bits) for bits in GZ_ORDER]
     tm_peers = [flip(k, bits) for bits in HALF_ORDER]
     late, place = lax.div(k, HALF), lax.rem(k, HALF)
-    twin = flip(k, HALF)
-    my_z, my_p = lax.div(place, 2), lax.rem(place, 2)
+    twin = flip(k, HALF + 4)
+
+    def owned(device):
+        at = lax.rem(device, HALF)
+        return at + late * (4 - 8 * lax.div(at, 4))
+
+    mine = owned(k)
+    my_z, my_p = lax.div(mine, 2), lax.rem(mine, 2)
     pending = []
 
     barrier = pltpu.get_barrier_semaphore()
     beside, across = [flip(k, 2), flip(k, 4)], [flip(k, 1)]
     for peer in beside + across:
         pl.semaphore_signal(barrier, inc=1, device_id={"tm": peer}, device_id_type=MESH)
-    for peer in gz_peers:
+    for peer in gz_peers[2:]:
         pl.semaphore_signal(barrier, inc=1, device_id={"gz": peer}, device_id_type=MESH)
 
     @pl.when(late == 0)
@@ -95,13 +101,14 @@
         vext[0, HALO + z] = plane.reshape(4, 16, NX).astype(BF16)
         lat_chunk[2 * z : 2 * z + 2] = plane.reshape(2, 4, NY, NX)
 
-    pl.semaphore_wait(barrier, len(GZ_ORDER) + len(beside + across) + late)
+    pl.semaphore_wait(barrier, len(GZ_ORDER) - 2 + len(beside + across) + late)
 
     def relay(turn, peers):
         for peer in peers:
             pl.semaphore_signal(relay_sem.at[turn], inc=1, device_id={"tm": peer}, device_id_type=MESH)
 
     relay(0, beside)
+    pl.semaphore_signal(relay_sem.at[3], inc=1, device_id={"gz": flip(g, 4)}, device_id_type=MESH)
 
     @pl.when(late == 1)
     def _():
@@ -259,11 +266,11 @@
 
     def middle(planes):
         rhs = stack(act, planes)
-        taps = jnp.dot(a_mid[...], rhs, preferred_element_type=F32)
+        taps = [jnp.dot(a_mid[256 * c : 256 * c + 256, :], rhs, preferred_element_type=F32) for c in range(3)]
         for i, r in enumerate(planes):
             summed[:, lanes(r)] = (
-                pltpu.roll(taps[0:256, lanes(i)], 1, 1) + taps[256:512, lanes(i)]
-                + pltpu.roll(taps[512:768, lanes(i)], NX - 1, 1) + splat[3] + lifted[:, lanes(r + 1)]
+                pltpu.roll(taps[0][:, lanes(i)], 1, 1) + taps[1][:, lanes(i)]
+                + pltpu.roll(taps[2][:, lanes(i)], NX - 1, 1) + splat[3] + lifted[:, lanes(r + 1)]
             )
 
     for sweep in range(2):
@@ -277,6 +284,7 @@
             settle(halo)
             turned(sweep, (2, 7))
             lift((2, 5))
+            pl.semaphore_wait(relay_sem.at[3], 1)
             copies = announce(lifted, (3, 4), (2, 5), centre, 0)
             pl.semaphore_wait(relay_sem.at[0], 2)
             relay(1, across)
@@ -322,9 +330,9 @@
             )
             send1[sweep, 2 * z : 2 * z + 2] = (step * predicted + drift[z]).reshape(2, 4, NY, NX)
 
-        chunk_a[sweep, place] = send1[sweep, place]
+        chunk_a[sweep, place] = send1[sweep, mine]
         copies = [
-            send(send1.at[sweep, lax.rem(peer, HALF)], chunk_a.at[sweep, place],
+            send(send1.at[sweep, owned(peer)], chunk_a.at[sweep, place],
                  p1_ss.at[sweep, i], p1_rs.at[sweep, i], {"tm": peer})
             for i, peer in enumerate(tm_peers)
         ]
@@ -347,7 +355,7 @@
         def _():
             onward().wait_recv()
 
-        state = lat_chunk[place] + earlier_sum[sweep]
+        state = lat_chunk[mine] + earlier_sum[sweep]
         for s in range(HALF):
             if sweep == 0:
                 chunk_b[s] = state.reshape(2, 16, NX).astype(BF16)
@@ -442,7 +450,7 @@
             pltpu.VMEM((HALF, 2, 16, NX), BF16),
             pltpu.VMEM((2, 4, NY, NX), F32),
             pltpu.VMEM((2, 4, NY, NX), F32),
-            pltpu.SemaphoreType.REGULAR((3,)), dma((15,)), dma((2, 2)), dma((2, 2)), dma((HALF,)), dma((4,)), dma((4, SIDE)), dma((4, SIDE)),
+            pltpu.SemaphoreType.REGULAR((4,)), dma((15,)), dma((2, 2)), dma((2, 2)), dma((HALF,)), dma((4,)), dma((4, SIDE)), dma((4, SIDE)),
             dma((2, HALF)), dma((2, HALF)), dma((2, HALF)), dma((2, HALF)), dma((2,)), dma((2,)),
         ],
         compiler_params=pltpu.CompilerParams(

time: 56.7 us -> 55.6 us (0.981)
  the two profiles are of different devices: /device:TPU:224 before, /device:TPU:1 now
where the time goes in v5:
time: 55.6 us; the launch traced here: 54.8 us
  Pallas kernels  52.8 us (95%)
  between operations  1.3 us (2%)
  local copies, waits for them, and re-layouts  0.66 us (1%)
    pallas_call x1, Pallas kernels, shards(): pl.pallas_call(kernel, out_shape=pltpu.VMEM((CH, NZ, NY, NX), F32), in_sp...  52.8 us

profile of v5, /device:TPU:1, one launch (start us, length us, event | category | flops | bytes accessed | tf_op | source)
XLA Modules:
  0.0 54.8 jit_solution(16587841800628891078)
XLA Ops:
  1.3 52.8 %shard_map.145 = f32[8,4,8,128]{3,2,1,0:T(8,128)S(1)} custom-call(f32[8,4,8,128]{3,2,1,0:T(8,128)} %lat_hbm.1, bf16[8,4,8,128]{3,2,1,0:T(8,128)(2,1)} %bitcast.13, f32[1,32]{1,0:T(1,128)} %emb_hbm.1, f32[1]{0:T(128)S(6)} %copy.18.step_hbm, f32[1]{0:T(128)S(6)} %copy.19.nsc_hbm, bf16[216,32]{1,0:T(8,128)(2,1)} %bitcast.14, f32[32]{0:T(128)} %bin_hbm.1, ...), custom_call_target="tpu_custom_call" | custom-call | tf_op jit(solution)/shard_map/pallas_call | solution.py:423
  54.1 0.7 %copy.17 = f32[1,8,4,8,128]{4,3,2,1,0:T(8,128)} copy(f32[1,8,4,8,128]{4,3,2,1,0:T(8,128)S(1)} %bitcast.11) | data formatting | bytes 262144

commit v6 on v5

--- a/solution.py
+++ b/solution.py
@@ -191,7 +191,8 @@
         return slice(NX * first, NX * (first + count))
 
     sub = lax.broadcasted_iota(jnp.int32, (8, NX), 0)
-    low = lax.broadcasted_iota(jnp.int32, (8, NX), 1) < NX // 2
+    lane = lax.broadcasted_iota(jnp.int32, (8, NX), 1)
+    own_lane, first_lane = lax.rem(lane, GR) == sub, lane == sub
 
     def lane_sums(groups):
         rows = jnp.concatenate([jnp.sum(t, axis=0, keepdims=True) for t in groups], axis=0)
@@ -219,9 +220,10 @@
         first = lane_sums([x + y for x, y in zip(plain, plain2)])
         second = lane_sums([x + y for x, y in zip(squares, squares2)])
         off = first * (1.0 / CELLS)
-        tile = jnp.where(low, centre + off, second - first * off)
-        stat[turn] = tile
-        recv[turn, g] = tile
+        both = jnp.where(lax.rem(lane, 2 * GR) < GR, centre + off, second - first * off)
+        row = jnp.sum(jnp.where(own_lane, both, 0.0), axis=0, keepdims=True)
+        stat[turn] = row
+        recv[turn, g] = row
         return [
             send(stat.at[turn], recv.at[turn, g], stat_ss.at[turn, i], stat_rs.at[turn, i], {"gz": peer})
             for i, peer in enumerate(gz_peers)
@@ -234,9 +236,13 @@
         mean = total * (1.0 / SIDE)
         off = every - mean[None]
         spread_of = jnp.sum(off * off, axis=0)
-        var = (pltpu.roll(total, NX // 2, 1) + spread_of * CELLS) * (1.0 / (CELLS * SIDE))
-        inv = lax.rsqrt(var + 1e-05)
-        return jnp.where(low, mean, pltpu.roll(mean, NX // 2, 1)), jnp.where(low, inv, pltpu.roll(inv, NX // 2, 1))
+        var = (pltpu.roll(total, NX - GR, 1) + spread_of * CELLS) * (1.0 / (CELLS * SIDE))
+
+        def by_row(row):
+            picked = jnp.where(first_lane, jnp.broadcast_to(row, (8, NX)), 0.0)
+            return jnp.broadcast_to(jnp.sum(picked, axis=1, keepdims=True), (8, NX))
+
+        return by_row(mean), by_row(lax.rsqrt(var + 1e-05))
 
     def activate(src, dst, planes, mean, inv, gain, shift):
         for gr in range(GR):
@@ -299,8 +305,9 @@
                      halo_ss.at[1, 1], halo_rs.at[1, 1], {"gz": down}),
             ]
             turned(sweep, (2, 3, 4, 5, 6, 7))
-            lift((2, 3, 4, 5))
+            lift((3, 4))
             centre = centre_of(lifted, (3, 4))
+            lift((2, 5))
             copies = announce(lifted, (3, 4), (2, 5), centre, 2)
             for copy in halo:
                 copy.wait_recv()
@@ -442,8 +449,8 @@
             pltpu.VMEM((6, 256, NX), F32),
             pltpu.VMEM((64, NX), F32),
             pltpu.VMEM((NZ, 64, NX), F32),
-            pltpu.VMEM((4, 8, NX), F32),
-            pltpu.VMEM((4, SIDE, 8, NX), F32),
+            pltpu.VMEM((4, 1, NX), F32),
+            pltpu.VMEM((4, SIDE, 1, NX), F32),
             pltpu.VMEM((3, HALF, 4, NY, NX), F32),
             pltpu.VMEM((HALF, 4, NY, NX), F32),
             pltpu.VMEM((2, HALF, 4, NY, NX), F32),

time: 55.6 us -> 55.2 us (level)
  Pallas kernels: 52.8 us -> 52.2 us
    pallas_call x1, Pallas kernels: 52.8 us -> 52.2 us  [shards(): pl.pallas_call(kernel, out_shape=pltpu.VMEM((CH, NZ, NY, NX), F32), in_sp...]
where the time goes in v6:
time: 55.2 us; the launch traced here: 54.1 us
  Pallas kernels  52.2 us (95%)
  between operations  1.3 us (2%)
  local copies, waits for them, and re-layouts  0.66 us (1%)
    pallas_call x1, Pallas kernels, shards(): pl.pallas_call(kernel, out_shape=pltpu.VMEM((CH, NZ, NY, NX), F32), in_sp...  52.2 us

profile of v6, /device:TPU:1, one launch (start us, length us, event | category | flops | bytes accessed | tf_op | source)
XLA Modules:
  0.0 54.1 jit_solution(14059852877939554618)
XLA Ops:
  1.3 52.2 %shard_map.145 = f32[8,4,8,128]{3,2,1,0:T(8,128)S(1)} custom-call(f32[8,4,8,128]{3,2,1,0:T(8,128)} %lat_hbm.1, bf16[8,4,8,128]{3,2,1,0:T(8,128)(2,1)} %bitcast.13, f32[1,32]{1,0:T(1,128)} %emb_hbm.1, f32[1]{0:T(128)S(6)} %copy.18.step_hbm, f32[1]{0:T(128)S(6)} %copy.19.nsc_hbm, bf16[216,32]{1,0:T(8,128)(2,1)} %bitcast.14, f32[32]{0:T(128)} %bin_hbm.1, ...), custom_call_target="tpu_custom_call" | custom-call | tf_op jit(solution)/shard_map/pallas_call | solution.py:430
  53.5 0.7 %copy.17 = f32[1,8,4,8,128]{4,3,2,1,0:T(8,128)} copy(f32[1,8,4,8,128]{4,3,2,1,0:T(8,128)S(1)} %bitcast.11) | data formatting | bytes 262144

commit v7 on v6

--- a/solution.py
+++ b/solution.py
@@ -383,11 +383,6 @@
                     device_id={"tm": peer, "gz": other}, device_id_type=MESH,
                 )
 
-            @pl.when(face)
-            def _():
-                for i, peer in enumerate(tm_peers + [k]):
-                    edge_copy(i, peer).start()
-
         for i, peer in enumerate(tm_peers):
             if sweep == 0:
                 src, dst = chunk_b.at[lax.rem(peer, HALF)], vext.at[1, HALO + my_z, pl.ds(2 * my_p, 2)]
@@ -395,6 +390,12 @@
                 src, dst = send1.at[2, lax.rem(peer, HALF)], out_ref.at[pl.ds(4 * my_p, 4), my_z]
             copies.append(send(src, dst, p2_ss.at[sweep, i], p2_rs.at[sweep, i], {"tm": peer}))
         if sweep == 0:
+
+            @pl.when(face)
+            def _():
+                for i, peer in enumerate(tm_peers + [k]):
+                    edge_copy(i, peer).start()
+
             vext[1, HALO + my_z, pl.ds(2 * my_p, 2)] = chunk_b[place]
         else:
             out_ref[pl.ds(4 * my_p, 4), my_z] = send1[2, place]

time: 55.2 us -> 55 us (level)
  no operation moved by 1% of the time
where the time goes in v7:
time: 55 us; the launch traced here: 54 us
  Pallas kernels  52 us (95%)
  between operations  1.3 us (2%)
  local copies, waits for them, and re-layouts  0.66 us (1%)
    pallas_call x1, Pallas kernels, shards(): pl.pallas_call(kernel, out_shape=pltpu.VMEM((CH, NZ, NY, NX), F32), in_sp...  52 us

profile of v7, /device:TPU:1, one launch (start us, length us, event | category | flops | bytes accessed | tf_op | source)
XLA Modules:
  0.0 54.0 jit_solution(3212340825892830721)
XLA Ops:
  1.3 52.0 %shard_map.145 = f32[8,4,8,128]{3,2,1,0:T(8,128)S(1)} custom-call(f32[8,4,8,128]{3,2,1,0:T(8,128)} %lat_hbm.1, bf16[8,4,8,128]{3,2,1,0:T(8,128)(2,1)} %bitcast.13, f32[1,32]{1,0:T(1,128)} %emb_hbm.1, f32[1]{0:T(128)S(6)} %copy.18.step_hbm, f32[1]{0:T(128)S(6)} %copy.19.nsc_hbm, bf16[216,32]{1,0:T(8,128)(2,1)} %bitcast.14, f32[32]{0:T(128)} %bin_hbm.1, ...), custom_call_target="tpu_custom_call" | custom-call | tf_op jit(solution)/shard_map/pallas_call | solution.py:431
  53.3 0.7 %copy.17 = f32[1,8,4,8,128]{4,3,2,1,0:T(8,128)} copy(f32[1,8,4,8,128]{4,3,2,1,0:T(8,128)S(1)} %bitcast.11) | data formatting | bytes 262144
